TPU v7x, 512 devices: a whole 4x8x8 slice. The times are simulated.
512 devices in a mesh: dp: 16 (over z_lo, x, core), tensor: 32 (over z_hi, y).
Axes of the slice: x: 4, y: 8, z: 8 (z_hi: 4, z_lo: 2; z = z_hi * 2 + z_lo), core: 2. Of those that a mesh axis runs over, the one named last changes fastest.
Arguments:
- attn_out: bfloat16 [4096, 8192], P('dp', 'tensor'), may hold values from -6 to 6
- teacher: bfloat16 [4096, 8192], P(('dp', 'tensor')), may hold values from -6 to 6
- int_codes: bfloat16 [8192, 8192], P(None, 'tensor'), may hold values from 0 to 15, as said below
- scales: float32 [64, 8192], P(None, 'tensor'), may hold values from 0.001 to 0.004
- offsets: float32 [64, 8192], P(None, 'tensor'), may hold values from 0.005 to 0.025
- lengths: int32 [32], replicated, may hold values from 1 to 128, 3072 in all
- shard_map: int32 [32], replicated, may hold values from 0 to 31, each once
Outputs:
- grad_scale: float32 [64, 8192], P(None, 'tensor')
- grad_offset: float32 [64, 8192], P(None, 'tensor')
Inputs may be any that keep to these rules, and one draw needn't show every extreme that they name: `int_codes`: whole numbers. `lengths`: at least one sequence is full; they sum to 3072. `shard_map`: each block number once.
All inputs are finite; a program needn't handle non-finite values.
Results may differ from a plain program's by a relative error of at most 0.0023.
Values may be sent and summed in bfloat16 or wider, within the bound.
A program may use at most 128 MiB of HBM per device.

v0:
```python
import jax
import jax.numpy as jnp
from jax import lax
from jax.sharding import PartitionSpec as P

SEQ = 128


def dequantize(int_codes, scales, offsets):
    group_count = scales.shape[0]
    in_rows = int_codes.shape[0]
    shaped = int_codes.astype(jnp.float32).reshape(group_count, in_rows // group_count, -1)
    return (
        (shaped * scales[:, None, :] - offsets[:, None, :])
        .reshape(in_rows, -1)
        .astype(jnp.bfloat16)
    )


def inverse_of(shard_map):
    indices = jnp.arange(shard_map.shape[0], dtype=jnp.int32)
    hits = (shard_map[:, None] == indices[None, :]).astype(jnp.int32)
    return jnp.sum(indices[:, None] * hits, axis=0)


def live_rows(seq_lengths):
    positions = jnp.arange(SEQ, dtype=jnp.int32)
    return (positions[None, :] < seq_lengths[:, None]).astype(jnp.float32).reshape(-1)


def reduce_groups(weight_grad, int_codes, group_count):
    shaped = weight_grad.reshape(group_count, -1, weight_grad.shape[1])
    codes_f = int_codes.astype(jnp.float32).reshape(shaped.shape)
    return (jnp.sum(shaped * codes_f, axis=1), -jnp.sum(shaped, axis=1))


def make_cotangent(student, target, live_mask, live_total):
    return (2.0 * (student - target.astype(jnp.float32)) * live_mask[:, None] / live_total).astype(
        jnp.bfloat16
    )


def per_device(attn_out, teacher, int_codes, scales, offsets, lengths, shard_map):
    weight = dequantize(int_codes, scales, offsets)
    columns = weight.shape[1]
    tok_rows = attn_out.shape[0]
    shard_count = lax.axis_size("tensor")
    seq_count = tok_rows // SEQ
    first_seq = lax.axis_index("dp") * seq_count
    live_mask = live_rows(lax.dynamic_slice_in_dim(lengths, first_seq, seq_count))
    live_total = jnp.sum(lengths).astype(jnp.float32)
    inverse = inverse_of(shard_map)
    everything = lax.all_gather(teacher, "tensor", axis=0, tiled=True)
    arrived = lax.dynamic_slice_in_dim(everything, lax.axis_index("tensor") * columns, columns, 1)
    target = jnp.take(arrived.reshape(shard_count, -1, columns), inverse, axis=0).reshape(
        tok_rows, columns
    )
    student = jnp.dot(
        lax.all_gather(attn_out, "tensor", axis=1, tiled=True),
        weight,
        preferred_element_type=jnp.float32,
    )
    cotangent = make_cotangent(student, target, live_mask, live_total)
    weight_grad = lax.dot_general(
        lax.all_gather(attn_out, "tensor", axis=1, tiled=True),
        cotangent,
        (((0,), (0,)), ((), ())),
        preferred_element_type=jnp.float32,
    )
    part_scale, part_offset = reduce_groups(weight_grad, int_codes, scales.shape[0])
    grad_scale, grad_offset = lax.psum((part_scale, part_offset), "dp")
    return (grad_scale, grad_offset)


def solution(mesh):
    in_specs = (
        P("dp", "tensor"),
        P(("dp", "tensor"), None),
        P(None, "tensor"),
        P(None, "tensor"),
        P(None, "tensor"),
        P(),
        P(),
    )
    out_specs = (P(None, "tensor"), P(None, "tensor"))
    return jax.shard_map(
        per_device, mesh=mesh, in_specs=in_specs, out_specs=out_specs, check_vma=False
    )
```

profile of v0, /device:TPU:1, one launch (start us, length us, event | category | flops | bytes accessed | tf_op | source)
XLA Modules:
  0.0 391.4 jit_solution(697624527876408787)
XLA Ops:
  7.2 0.0 all-gather.5.cloned.1.call-start
  7.2 0.7 all-gather.5.cloned.1.call-update
  7.9 0.0 all-gather.3.cloned.1.call-start
  7.9 0.7 all-gather.3.cloned.1.call-update
  8.6 0.0 all-reduce.3.cloned.1.call-start
  8.7 1.3 reduce_sum.40
  10.6 0.7 dynamic_slice.7
  11.4 0.7 select_reduce_fusion
  12.1 0.1 broadcast_in_dim.21
  12.2 0.1 broadcast_in_dim.22
  12.3 0.0 copy-start
  12.3 0.0 copy-start.1
  12.3 7.1 %copy.19 = f32[64,128,256]{1,0,2:T(8,128)} copy(bf16[64,128,256]{2,1,0:T(8,128)(2,1)} %bitcast.41) | data formatting | bytes 12582912 | tf_op jit(solution)/shard_map/reshape | solution.py:12
  19.4 0.0 copy-done
  19.4 0.0 copy-done.1
  19.4 5.2 %fusion = bf16[8192,256]{1,0:T(8,128)(2,1)} fusion(f32[64,256]{1,0:T(8,128)S(1)} %copy-done, f32[64,256]{1,0:T(8,128)S(1)} %copy-done.1, bf16[8192,256]{1,0:T(8,128)(2,1)} %param.9), kind=kLoop, calls=%fused_computation.2 | loop fusion | flops 8388608 | bytes 8519680 | tf_op jit(solution)/shard_map/convert_element_type | solution.py:16
  24.6 0.1 fusion.11
  24.7 94.1 %all-gather.5.cloned.1.call-done = bf16[256,8192]{1,0:T(8,128)(2,1)} async-done(((bf16[8,8192]{1,0:T(8,128)(2,1)}), bf16[256,8192]{1,0:T(8,128)(2,1)}) %all-gather.5.cloned.1.call-update) | async-done | bytes 4194320 | tf_op jit(solution)/shard_map/all_gather | solution.py:53
  118.8 0.9 dynamic-slice_bitcast_fusion
  119.7 0.6 gather_fusion
  120.3 0.1 copy.18
  120.4 106.1 %all-gather.3.cloned.1.call-done = bf16[256,8192]{1,0:T(8,128)(2,1)} async-done(((bf16[256,256]{1,0:T(8,128)(2,1)}), bf16[256,8192]{1,0:T(8,128)(2,1)}) %all-gather.3.cloned.1.call-update) | async-done | bytes 4194320 | tf_op jit(solution)/shard_map/all_gather | solution.py:65
  226.6 12.4 %convolution_bitcast_fusion = f32[32,8,64,128]{3,1,2,0:T(8,128)} fusion(bf16[256,8192]{1,0:T(8,128)(2,1)} %all-gather.3.cloned.1.call-done, bf16[8192,256]{1,0:T(8,128)(2,1)} %fusion, f32[]{:T(128)S(6)} %convert_element_type.25, f32[256]{0:T(256)S(1)} %fusion.11, bf16[256,256]{0,1:T(8,128)(2,1)S(1)} %copy.18, pred[256]{0:T(512)(128)(4,1)S(1)} %broadcast_in_dim.22), kind=kOutput, calls=%fused_computation.5 | convolution fusion | flops 2147876864 | bytes 16909572 | tf_op jit(solution)/shard_map/dot_general | solution.py:64
  239.0 8.2 %copy.22 = f32[32,8,64,128]{3,2,1,0:T(8,128)} copy(f32[32,8,64,128]{3,1,2,0:T(8,128)} %convolution_bitcast_fusion) | data formatting | bytes 16777216
  247.2 10.8 %fusion.14 = (f32[64,256]{0,1:T(8,128)S(1)}, f32[64,256]{0,1:T(8,128)}) fusion(f32[64,128,256]{1,0,2:T(8,128)} %bitcast.40, f32[64,128,256]{1,0,2:T(8,128)} %copy.19), kind=kLoop, calls=%fused_computation.28 | loop fusion | flops 6258688 | bytes 16908288 | tf_op jit(solution)/shard_map/reduce_sum | solution.py:34
  258.1 0.7 neg.3
  258.7 0.0 all-reduce.3.cloned.1.call-update
  258.8 122.8 %all-reduce.3.cloned.1.call-done = (f32[64,256]{0,1:T(8,128)}, f32[64,256]{0,1:T(8,128)}) async-done(((f32[64,256]{0,1:T(8,128)}, f32[64,256]{0,1:T(8,128)}), (f32[64,256]{0,1:T(8,128)}, f32[64,256]{0,1:T(8,128)})) %all-reduce.3.cloned.1.call-update) | async-done | bytes 131088 | tf_op jit(solution)/shard_map/psum | solution.py:71
  381.6 1.6 copy.20
  383.2 1.6 copy.21
  (3 shorter events, 0.0 us)
Async XLA Ops:
  7.2 111.7 %all-gather.5.cloned.1.call-start = ((), (), s32[]{:S(2)}) async-start(), calls=%async_computation.1 | async-start | bytes 4325376 | tf_op jit(solution)/shard_map/all_gather | solution.py:53
  7.9 218.7 %all-gather.3.cloned.1.call-start = ((), (), s32[]{:S(2)}) async-start(), calls=%async_computation | async-start | bytes 4325376 | tf_op jit(solution)/shard_map/all_gather | solution.py:65
  8.6 372.9 %all-reduce.3.cloned.1.call-start = ((), (), s32[]{:S(2)}) async-start(), calls=%async_computation.2 | async-start | bytes 524288 | tf_op jit(solution)/shard_map/psum | solution.py:71
  12.3 7.1 %copy-start = (f32[64,256]{1,0:T(8,128)S(1)}, f32[64,256]{1,0:T(8,128)}, u32[]{:S(2)}) copy-start(f32[64,256]{1,0:T(8,128)} %param.11) | copy-start | bytes 196612
  12.3 7.1 %copy-start.1 = (f32[64,256]{1,0:T(8,128)S(1)}, f32[64,256]{1,0:T(8,128)}, u32[]{:S(2)}) copy-start(f32[64,256]{1,0:T(8,128)} %param.10) | copy-start | bytes 196612
Sparse Core Ops, SparseCore 0:
  11.2 107.6 all-gather.4
  121.9 104.6 all-gather.2
  258.9 122.6 all-reduce.2
where the time goes:
time: 392 us; the launch traced here: 391 us
  waiting for transfers between devices  324 us (83%)
  local copies, waits for them, and re-layouts  21 us (5%)
  other arithmetic  18.8 us (5%)
  between operations  14.4 us (4%)
  matrix products  12.4 us (3%)
    psum x1, waiting for transfers between devices, per_device(): grad_scale, grad_offset = lax.psum((part_scale, part_offset), 'dp')  123 us
    all_gather x1, waiting for transfers between devices, per_device(): lax.all_gather(attn_out, 'tensor', axis=1, tiled=True)  106 us
    all_gather x1, waiting for transfers between devices, per_device(): everything = lax.all_gather(teacher, 'tensor', axis=0, tiled=True)  94.1 us
    dot_general x1, matrix products, per_device(): lax.dot_general(lax.all_gather(attn_out, 'tensor', axis=1, tiled=True), c...  12.4 us
    unnamed x7, local copies, waits for them, and re-layouts  11.5 us
    reduce_sum x1, other arithmetic, reduce_groups(): return (jnp.sum(shaped * codes_f, axis=1), -jnp.sum(shaped, axis=1))  10.8 us
  transfers between devices with their start and end apart: 3, of which 3 were waited for; matrix products, arithmetic and copies ran while one was open for 4% of the time, Pallas kernels for 0%

commit v1 on v0

v1 whole, which is shorter than its diff:
```python
import functools

import jax
import jax.numpy as jnp
from jax import lax
from jax.experimental import pallas as pl
from jax.experimental.pallas import tpu as pltpu
from jax.sharding import PartitionSpec as P

SEQ = 128
R1 = 160
R2 = 96
H1, H2 = R1 // 2, R2 // 2
T = R1 + R2
NY, NZ = 8, 4
NT = NY * NZ
NDP = 16
C = 256
GROUPS = 64
F32, BF16 = jnp.float32, jnp.bfloat16
MESH = pl.DeviceIdType.MESH


def kernel(
    lengths, shard_map, attn, teacher, codes_hbm, scales, offsets, out,
    a1, a2, codes, weight, parts, acc, rowsum, t_land, target, grads, rs_land,
    loc_sem, y1s, y1r, z1s, z1r, y2s, y2r, z2s, z2r, ts, tr, rss, rsr, ags, agr,
):
    dp = lax.axis_index("dp")
    me = lax.axis_index("tensor")
    zh, y = me // NY, me % NY

    def slot_of(z, yy):
        return z * NY + yy

    def dev(z, yy):
        return (dp, slot_of(z, yy))

    y_nb = (dev(zh, (y + 1) % NY), dev(zh, (y + NY - 1) % NY))
    z_nb = (dev((zh + 1) % NZ, y), dev((zh + NZ - 1) % NZ, y))

    def remote(src, dst, ssem, rsem, to):
        return pltpu.make_async_remote_copy(
            src_ref=src, dst_ref=dst, send_sem=ssem, recv_sem=rsem,
            device_id=to, device_id_type=MESH,
        )

    loc = [
        pltpu.make_async_copy(attn.at[pl.ds(0, R1)], a1.at[me], loc_sem.at[0]),
        pltpu.make_async_copy(attn.at[pl.ds(R1, R2)], a2.at[me], loc_sem.at[1]),
        pltpu.make_async_copy(codes_hbm, codes, loc_sem.at[2]),
        pltpu.make_async_copy(
            teacher.at[:, pl.ds(pl.multiple_of(me * C, C), C)], t_land.at[me], loc_sem.at[3]
        ),
    ]
    for c in loc:
        c.start()

    barrier = pltpu.get_barrier_semaphore()

    @pl.loop(1, NT)
    def _(i):
        pl.semaphore_signal(barrier, 1, device_id=(dp, (me + i) % NT), device_id_type=MESH)

    @pl.loop(1, NDP)
    def _(i):
        pl.semaphore_signal(barrier, 1, device_id=((dp + i) % NDP, me), device_id_type=MESH)

    pl.semaphore_wait(barrier, NT - 1 + NDP - 1)
    loc[0].wait()
    loc[1].wait()

    def z1_full(d):
        src = slot_of(zh, y)
        return remote(a1.at[src], a1.at[src], z1s.at[d], z1r.at[d], z_nb[d])

    def z1_half(d):
        src = slot_of((zh + (NZ - 1 if d == 0 else 1)) % NZ, y)
        ref = a1.at[src, pl.ds(d * H1, H1)]
        return remote(ref, ref, z1s.at[2 + d], z1r.at[2 + d], z_nb[d])

    def y1_slot(s, k, d):
        off = k + k // 2 - 2 * (k // 3)
        yy = (y + NY - s) % NY if d == 0 else (y + s) % NY
        return slot_of((zh + off) % NZ, yy)

    def y1_full(s, k, d):
        ref = a1.at[y1_slot(s, k, d)]
        return remote(ref, ref, y1s.at[s, k, d], y1r.at[s, k, d], y_nb[d])

    def y1_half(k, d):
        ref = a1.at[y1_slot(3, k, d), pl.ds(d * H1, H1)]
        return remote(ref, ref, y1s.at[3, k, d], y1r.at[3, k, d], y_nb[d])

    def y2_slot(s, d):
        return slot_of(zh, (y + NY - s) % NY if d == 0 else (y + s) % NY)

    def y2_full(s, d):
        ref = a2.at[y2_slot(s, d)]
        return remote(ref, ref, y2s.at[s, d], y2r.at[s, d], y_nb[d])

    def y2_half(d):
        ref = a2.at[y2_slot(3, d), pl.ds(d * H2, H2)]
        return remote(ref, ref, y2s.at[3, d], y2r.at[3, d], y_nb[d])

    def y_of(m):
        dist = (m + 1) // 2
        odd = m % 2
        return (y + NY + dist * (1 - 2 * odd)) % NY

    def z2_full(m, d):
        ref = a2.at[slot_of(zh, y_of(m))]
        return remote(ref, ref, z2s.at[m, d], z2r.at[m, d], z_nb[d])

    def z2_half(m, d):
        src = slot_of((zh + (NZ - 1 if d == 0 else 1)) % NZ, y_of(m))
        ref = a2.at[src, pl.ds(d * H2, H2)]
        return remote(ref, ref, z2s.at[m, 2 + d], z2r.at[m, 2 + d], z_nb[d])

    for d in range(2):
        z1_full(d).start()
        y2_full(0, d).start()
        y1_full(0, 0, d).start()
        z2_full(0, d).start()

    def t_copy(i):
        to = (me + i) % NT
        return remote(
            teacher.at[:, pl.ds(pl.multiple_of(to * C, C), C)], t_land.at[me],
            ts.at[i], tr.at[i], (dp, to),
        )

    @pl.loop(1, NT)
    def _(i):
        t_copy(i).start()

    loc[2].wait()
    acc[...] = jnp.zeros_like(acc)
    rowsum[...] = jnp.zeros_like(rowsum)

    @pl.loop(0, GROUPS)
    def _(g):
        rows = pl.ds(pl.multiple_of(g * 128, 128), 128)
        weight[rows, :] = (
            codes[rows, :].astype(F32) * scales[pl.ds(g, 1), :] - offsets[pl.ds(g, 1), :]
        ).astype(BF16)

    group_iota = lax.broadcasted_iota(jnp.int32, (GROUPS, C), 0)
    feat_half = lax.broadcasted_iota(jnp.int32, (GROUPS, C), 1) // 128

    def use(a, slot, first, rows):
        at = pl.ds(first, rows)
        k0 = pl.ds(pl.multiple_of(slot * C, C), C)
        ka = pl.ds(pl.multiple_of(slot * C, C), 128)
        kb = pl.ds(pl.multiple_of(slot * C + 128, 128), 128)
        acc[at, :] += jnp.dot(a, weight[k0, :], preferred_element_type=F32)
        parts[2 * slot, at, :] = jnp.dot(a[:, :128], codes[ka, :], preferred_element_type=F32)
        parts[2 * slot + 1, at, :] = jnp.dot(a[:, 128:], codes[kb, :], preferred_element_type=F32)
        pick = (group_iota == 2 * slot + feat_half).astype(BF16)
        pad = jnp.zeros((T - rows, C), BF16)
        whole = jnp.concatenate([a, pad] if first == 0 else [pad, a], axis=0)
        rowsum[...] += lax.dot_general(
            pick, whole, (((1,), (1,)), ((), ())), preferred_element_type=F32
        )

    def use1(slot):
        use(a1[slot], slot, 0, R1)

    def use2(slot):
        use(a2[slot], slot, R1, R2)

    def make_target():
        loc[3].wait()

        @pl.loop(1, NT)
        def _(i):
            t_copy(i).wait_recv()

        lane = lax.broadcasted_iota(jnp.int32, (8, T), 1)
        where_to = jnp.zeros((8, T), jnp.int32)
        for j in range(NT):
            where_to = jnp.where(lane // 8 == j, shard_map[j] * 8 + lane % 8, where_to)
        row = lax.broadcasted_iota(jnp.int32, (T, T), 0)
        perm = (row == where_to[:1, :]).astype(F32).astype(BF16)
        arrived = t_land[...].astype(F32).reshape(T, C).astype(BF16)
        target[...] = jnp.dot(perm, arrived, preferred_element_type=F32)

    LAG1, LAG2 = 6, 12

    @pl.loop(0, 20)
    def _(n):
        s, k = n // 4, n % 4

        @pl.when(s == 0)
        def _():
            @pl.when(k == 1)
            def _():
                z1_full(1).wait_recv()
                z1_half(1).start()

            @pl.when(k == 2)
            def _():
                z1_full(0).wait_recv()
                z1_half(0).start()

            @pl.when(k == 3)
            def _():
                z1_half(0).wait_recv()
                z1_half(1).wait_recv()

            @pl.when(k > 0)
            def _():
                y1_full(0, k, 0).start()
                y1_full(0, k, 1).start()

        for sv in (1, 2):
            @pl.when(s == sv)
            def _():
                for d in range(2):
                    y1_full(sv - 1, k, d).wait_recv()
                    y1_full(sv, k, d).start()

        @pl.when(s == 3)
        def _():
            for d in range(2):
                y1_full(2, k, d).wait_recv()
                y1_half(k, d).start()

        @pl.when(s == 4)
        def _():
            for d in range(2):
                y1_half(k, d).wait_recv()

        m = n

        @pl.when((m >= 1) & (m <= 7))
        def _():
            dist = (m + 1) // 2
            for d in range(2):
                @pl.when((m % 2 == 1 - d) & (m < 7))
                def _():
                    y2_full(dist - 1, d).wait_recv()

                    @pl.when(dist < 3)
                    def _():
                        y2_full(dist, d).start()

                    @pl.when(dist == 3)
                    def _():
                        y2_half(d).start()

            @pl.when(m == 7)
            def _():
                y2_half(0).wait_recv()
                y2_half(1).wait_recv()

            z2_full(m, 0).start()
            z2_full(m, 1).start()

        m1 = n - LAG1

        @pl.when((m1 >= 0) & (m1 < 8))
        def _():
            for d in range(2):
                z2_full(m1, d).wait_recv()
                z2_half(m1, d).start()

        m2 = n - LAG2

        @pl.when(m2 >= 0)
        def _():
            for d in range(2):
                z2_half(m2, d).wait_recv()

        use1(y1_slot(s, k, 0))

        @pl.when((s > 0) & (s < 4))
        def _():
            use1(y1_slot(s, k, 1))

        count = (m < 8).astype(jnp.int32) + 2 * ((m1 >= 0) & (m1 < 8)).astype(jnp.int32)

        @pl.when(m < 8)
        def _():
            use2(slot_of(zh, y_of(m)))

        @pl.when((m1 >= 0) & (m1 < 8))
        def _():
            @pl.loop(0, 2)
            def _(d):
                use2(slot_of((zh + 1 + 2 * d) % NZ, y_of(m1)))

        @pl.when(m2 >= 0)
        def _():
            use2(slot_of((zh + 2) % NZ, y_of(m2)))

        @pl.when(n == 14)
        def _():
            make_target()

    total = lengths[0]
    for i in range(1, 32):
        total = total + lengths[i]
    token = lax.broadcasted_iota(jnp.int32, (T, C), 0)
    limit = jnp.where(token < SEQ, lengths[2 * dp], lengths[2 * dp + 1] + SEQ)
    live = (token < limit).astype(F32)
    cot16 = (2.0 * (acc[...] - target[...]) * live / total.astype(F32)).astype(BF16)
    acc[...] = cot16.astype(F32)

    rs = rowsum[...]
    hi = rs.astype(BF16)
    rest = rs - hi.astype(F32)
    mid = rest.astype(BF16)
    low = (rest - mid.astype(F32)).astype(BF16)
    offs = jnp.dot(hi, cot16, preferred_element_type=F32)
    offs += jnp.dot(mid, cot16, preferred_element_type=F32)
    offs += jnp.dot(low, cot16, preferred_element_type=F32)
    grads[pl.ds(8, 8)] = -offs.reshape(8, 8, C)

    def rs_copy(c):
        return remote(grads.at[c], rs_land.at[dp], rss.at[c], rsr.at[dp], (c, me))

    def rs_wait(src):
        return remote(grads.at[src], rs_land.at[src], rss.at[src], rsr.at[src], (src, me))

    @pl.loop(8, 16)
    def _(c):
        @pl.when(c != dp)
        def _():
            rs_copy(c).start()

    @pl.loop(0, 8)
    def _(c):
        for q in range(8):
            prod = parts[c * 8 + q] * acc[...]
            grads[c, pl.ds(q, 1), :] = jnp.sum(prod, axis=0, keepdims=True)

        @pl.when(c != dp)
        def _():
            rs_copy(c).start()

    rs_land[dp] = grads[dp]

    @pl.loop(0, NDP)
    def _(c):
        @pl.when(c != dp)
        def _():
            rs_wait(c).wait_recv()

    out[dp] = jnp.sum(rs_land[...], axis=0)

    def ag_copy(c):
        return remote(out.at[dp], out.at[dp], ags.at[c], agr.at[dp], (c, me))

    def ag_wait(src):
        return remote(out.at[src], out.at[src], ags.at[src], agr.at[src], (src, me))

    @pl.loop(0, NDP)
    def _(c):
        @pl.when(c != dp)
        def _():
            ag_copy(c).start()

    for d in range(2):
        z1_full(d).wait_send()
        z1_half(d).wait_send()
        y2_half(d).wait_send()

        @pl.loop(0, 4)
        def _(k):
            for s in range(3):
                y1_full(s, k, d).wait_send()
            y1_half(k, d).wait_send()

        for s in range(3):
            y2_full(s, d).wait_send()

        @pl.loop(0, 8)
        def _(m):
            z2_full(m, d).wait_send()
            z2_half(m, d).wait_send()

    @pl.loop(1, NT)
    def _(i):
        t_copy(i).wait_send()

    @pl.loop(0, NDP)
    def _(c):
        @pl.when(c != dp)
        def _():
            rs_copy(c).wait_send()
            ag_wait(c).wait_recv()
            ag_copy(c).wait_send()


def per_device(attn_out, teacher, int_codes, scales, offsets, lengths, shard_map):
    dma = pltpu.SemaphoreType.DMA
    vmem = pl.BlockSpec(memory_space=pltpu.VMEM)
    smem = pl.BlockSpec(memory_space=pltpu.SMEM)
    hbm = pl.BlockSpec(memory_space=pl.ANY)
    out = pl.pallas_call(
        kernel,
        out_shape=jax.ShapeDtypeStruct((NDP, 8, C), F32),
        in_specs=[smem, smem, hbm, hbm, hbm, vmem, vmem],
        out_specs=vmem,
        scratch_shapes=[
            pltpu.VMEM((NT, R1, C), BF16),
            pltpu.VMEM((NT, R2, C), BF16),
            pltpu.VMEM((8192, C), BF16),
            pltpu.VMEM((8192, C), BF16),
            pltpu.VMEM((GROUPS, T, C), F32),
            pltpu.VMEM((T, C), F32),
            pltpu.VMEM((GROUPS, T), F32),
            pltpu.VMEM((NT, 8, C), BF16),
            pltpu.VMEM((T, C), F32),
            pltpu.VMEM((NDP, 8, C), F32),
            pltpu.VMEM((NDP, 8, C), F32),
            dma((4,)),
            dma((4, 4, 2)), dma((4, 4, 2)),
            dma((4,)), dma((4,)),
            dma((4, 2)), dma((4, 2)),
            dma((8, 4)), dma((8, 4)),
            dma((NT,)), dma((NT,)),
            dma((NDP,)), dma((NDP,)),
            dma((NDP,)), dma((NDP,)),
        ],
        compiler_params=pltpu.CompilerParams(
            collective_id=0, has_side_effects=True, vmem_limit_bytes=48 << 20
        ),
        cost_estimate=pl.CostEstimate(
            flops=3 * 2 * T * 8192 * C, bytes_accessed=6 << 20, transcendentals=0
        ),
    )(lengths, shard_map, attn_out, teacher, int_codes, scales, offsets)
    flat = out.reshape(128, C)
    return flat[:64], flat[64:]


def solution(mesh):
    in_specs = (
        P("dp", "tensor"),
        P(("dp", "tensor"), None),
        P(None, "tensor"),
        P(None, "tensor"),
        P(None, "tensor"),
        P(),
        P(),
    )
    out_specs = (P(None, "tensor"), P(None, "tensor"))
    return jax.shard_map(
        per_device, mesh=mesh, in_specs=in_specs, out_specs=out_specs, check_vma=False
    )
```

time: 392 us -> 79.5 us (0.20)
  waiting for transfers between devices: 324 us -> 0 us
  Pallas kernels: 0 us -> 71 us
  other arithmetic: 18.8 us -> 0 us
  between operations: 14.4 us -> 0.65 us
  local copies, waits for them, and re-layouts: 21 us -> 7.63 us
  matrix products: 12.4 us -> 0 us
    all_gather x2 -> x0, waiting for transfers between devices: 200 us -> none  [the longest x1 106 us: per_device(): lax.all_gather(attn_out, 'tensor', axis=1, tiled=True)]
    psum x1 -> x0, waiting for transfers between devices: 123 us -> none  [per_device(): grad_scale, grad_offset = lax.psum((part_scale, part_offset), 'dp')]
    pallas_call x0 -> x1, Pallas kernels: none -> 71 us  [per_device(): pl.pallas_call(kernel, out_shape=jax.ShapeDtypeStruct((NDP, 8, C), F32),...]
    reduce_sum x3 -> x0, other arithmetic: 12.9 us -> none  [the longest x1 10.8 us: reduce_groups(): return (jnp.sum(shaped * codes_f, axis=1), -jnp.sum(shaped, axis=1))]
    dot_general x1 -> x0, matrix products: 12.4 us -> none  [per_device(): lax.dot_general(lax.all_gather(attn_out, 'tensor', axis=1, tiled=True), c...]
    reshape x2 -> x0, local copies, waits for them, and re-layouts: 7.97 us -> none  [the longest x1 7.06 us: dequantize(): int_codes.astype(jnp.float32)]
    convert_element_type x1 -> x0, other arithmetic: 5.22 us -> none  [dequantize(): return (shaped * scales[:, None, :] - offsets[:, None, :]).reshape(in_row...]
    unnamed x7 -> x14, local copies, waits for them, and re-layouts: 11.5 us -> 6.98 us
  transfers between devices with their start and end apart: 3 -> 0, of which waited for: 3 -> 0; matrix products, arithmetic and copies ran while one was open for 4% -> 0% of each run, Pallas kernels for 0% -> 0%
where the time goes in v1:
time: 79.5 us; the launch traced here: 79.2 us
  Pallas kernels  71 us (89%)
  local copies, waits for them, and re-layouts  7.63 us (10%)
    pallas_call x1, Pallas kernels, per_device(): pl.pallas_call(kernel, out_shape=jax.ShapeDtypeStruct((NDP, 8, C), F32),...  71 us
    unnamed x14, local copies, waits for them, and re-layouts  6.98 us

profile of v1, /device:TPU:1, one launch (start us, length us, event | category | flops | bytes accessed | tf_op | source)
XLA Modules:
  0.0 79.2 jit_solution(936621962612747095)
XLA Ops:
  0.6 0.0 copy-start
  0.6 2.2 %copy-done = bf16[8192,256]{1,0:T(8,128)(2,1)S(1)} copy-done((bf16[8192,256]{1,0:T(8,128)(2,1)S(1)}, bf16[8192,256]{1,0:T(8,128)(2,1)}, u32[]{:S(2)}) %copy-start) | copy-done | bytes 4194328
  2.8 0.0 copy-start.1
  2.8 0.9 %copy-done.1 = bf16[256,256]{1,0:T(8,128)(2,1)S(1)} copy-done((bf16[256,256]{1,0:T(8,128)(2,1)S(1)}, bf16[256,256]{1,0:T(8,128)(2,1)}, u32[]{:S(2)}) %copy-start.1) | copy-done | bytes 131096
  3.7 0.0 copy-start.2
  3.7 0.9 %copy-done.2 = bf16[8,8192]{1,0:T(8,128)(2,1)S(1)} copy-done((bf16[8,8192]{1,0:T(8,128)(2,1)S(1)}, bf16[8,8192]{1,0:T(8,128)(2,1)}, u32[]{:S(2)}) %copy-start.2) | copy-done | bytes 131096
  4.6 0.0 copy-start.3
  4.6 0.8 %copy-done.3 = f32[64,256]{1,0:T(8,128)S(1)} copy-done((f32[64,256]{1,0:T(8,128)S(1)}, f32[64,256]{1,0:T(8,128)}, u32[]{:S(2)}) %copy-start.3) | copy-done | bytes 65560
  5.5 0.0 copy-start.4
  5.5 0.8 %copy-done.4 = f32[64,256]{1,0:T(8,128)S(1)} copy-done((f32[64,256]{1,0:T(8,128)S(1)}, f32[64,256]{1,0:T(8,128)}, u32[]{:S(2)}) %copy-start.4) | copy-done | bytes 65560
  6.3 0.0 copy-start.5
  6.3 0.7 copy-done.5
  7.0 0.0 copy-start.6
  7.0 0.7 copy-done.6
  7.6 71.0 %shard_map.87 = f32[16,8,256]{2,1,0:T(8,128)S(1)} custom-call(s32[32]{0:T(128)S(1)} %copy-done.5, s32[32]{0:T(128)S(1)} %copy-done.6, bf16[256,256]{1,0:T(8,128)(2,1)S(1)} %copy-done.1, bf16[8,8192]{1,0:T(8,128)(2,1)S(1)} %copy-done.2, bf16[8192,256]{1,0:T(8,128)(2,1)S(1)} %copy-done, f32[64,256]{1,0:T(8,128)S(1)} %copy-done.3, f32[64,256]{1,0:T(8,128)S(1)} %copy-done.4), custom_call_target="tpu_custom_call" | custom-call | flops 3221225472 | bytes 6291456 | tf_op jit(solution)/shard_map/pallas_call | solution.py:401
  78.6 0.7 slice_bitcast_fusion
Async XLA Ops:
  0.6 2.2 %copy-start = (bf16[8192,256]{1,0:T(8,128)(2,1)S(1)}, bf16[8192,256]{1,0:T(8,128)(2,1)}, u32[]{:S(2)}) copy-start(bf16[8192,256]{1,0:T(8,128)(2,1)} %codes_hbm.1) | copy-start | bytes 12582916
  2.8 0.9 %copy-start.1 = (bf16[256,256]{1,0:T(8,128)(2,1)S(1)}, bf16[256,256]{1,0:T(8,128)(2,1)}, u32[]{:S(2)}) copy-start(bf16[256,256]{1,0:T(8,128)(2,1)} %attn.1) | copy-start | bytes 393220
  3.7 0.9 %copy-start.2 = (bf16[8,8192]{1,0:T(8,128)(2,1)S(1)}, bf16[8,8192]{1,0:T(8,128)(2,1)}, u32[]{:S(2)}) copy-start(bf16[8,8192]{1,0:T(8,128)(2,1)} %teacher.1) | copy-start | bytes 393220
  4.6 0.8 %copy-start.3 = (f32[64,256]{1,0:T(8,128)S(1)}, f32[64,256]{1,0:T(8,128)}, u32[]{:S(2)}) copy-start(f32[64,256]{1,0:T(8,128)} %scales.1) | copy-start | bytes 196612
  5.5 0.8 %copy-start.4 = (f32[64,256]{1,0:T(8,128)S(1)}, f32[64,256]{1,0:T(8,128)}, u32[]{:S(2)}) copy-start(f32[64,256]{1,0:T(8,128)} %offsets.1) | copy-start | bytes 196612
  6.3 0.7 copy-start.5
  7.0 0.7 copy-start.6

commit v2 on v1

v2 whole, which is shorter than its diff:
```python
import functools

import jax
import jax.numpy as jnp
from jax import lax
from jax.experimental import pallas as pl
from jax.experimental.pallas import tpu as pltpu
from jax.sharding import PartitionSpec as P

SEQ = 128
R1 = 160
R2 = 96
H1, H2 = R1 // 2, R2 // 2
T = R1 + R2
NY, NZ = 8, 4
NT = NY * NZ
NDP = 16
C = 256
GROUPS = 64
F32, BF16 = jnp.float32, jnp.bfloat16
MESH = pl.DeviceIdType.MESH
PART1 = [
    (0, 0), (1, 0), (0, 1), (0, 2), (2, 0), (1, 1), (1, 2), (0, 3), (3, 0), (2, 1),
    (2, 2), (1, 3), (3, 1), (3, 2), (4, 0), (2, 3), (4, 1), (4, 2), (3, 3), (4, 3),
]
PART2_Y = [0, 1, 2, -1, 3, 4, -1, 5, 6, -1, 7, -1, -1, -1, -1, -1, -1, -1, -1, -1]
PART2_Z = [-1, -1, -1, -1, 0, -1, 1, -1, 2, -1, 3, -1, 4, -1, 5, -1, 6, 7, -1, -1]
PART2_ZZ = [-1, -1, -1, -1, -1, -1, -1, -1, -1, 0, -1, 1, -1, 2, -1, 3, 4, 5, 6, 7]


def kernel(
    lengths_hbm, shard_map_hbm, attn, teacher, codes_hbm, scales_hbm, offsets_hbm, out,
    lengths, shard_map, scales, offsets, a1, a2, codes, weight, parts, acc, rowsum, tz_land, t_land, target, grads, rs_land,
    loc_sem, a1s, a2s, y1r, z1r, y2r, y2hr, z2r, z2hr, tzs, tzr, tys, tyr, hello, rss, rsr, ags, agr,
):
    dp = lax.axis_index("dp")
    me = lax.axis_index("tensor")
    zh, y = me // NY, me % NY

    def slot_of(z, yy):
        return z * NY + yy

    def dev(z, yy):
        return (dp, slot_of(z, yy))

    y_nb = (dev(zh, (y + 1) % NY), dev(zh, (y + NY - 1) % NY))
    z_nb = (dev((zh + 1) % NZ, y), dev((zh + NZ - 1) % NZ, y))

    def remote(src, dst, ssem, rsem, to):
        return pltpu.make_async_remote_copy(
            src_ref=src, dst_ref=dst, send_sem=ssem, recv_sem=rsem,
            device_id=to, device_id_type=MESH,
        )

    def wait_all(ref, sem):
        pltpu.make_async_copy(ref, ref, sem).wait()

    zl, x, core = dp // 8, dp // 2 % 4, dp % 2

    def peer(zl_, x_, core_):
        return (zl_ * 8 + x_ * 2 + core_, me)

    dp_nb = (
        peer(zl, x, 1 - core), peer(1 - zl, x, core),
        peer(zl, (x + 1) % 4, core), peer(zl, (x + 3) % 4, core),
    )
    barrier = pltpu.get_barrier_semaphore()
    for to in y_nb + z_nb + dp_nb:
        pl.semaphore_signal(barrier, 1, device_id=to, device_id_type=MESH)

    def say_hello(r):
        for to in dp_nb:
            pl.semaphore_signal(hello.at[r], 1, device_id=to, device_id_type=MESH)

    def hear_hello(r):
        pl.semaphore_wait(hello.at[r], 4)

    loc = [
        pltpu.make_async_copy(attn.at[pl.ds(0, R1)], a1.at[me], loc_sem.at[0]),
        pltpu.make_async_copy(attn.at[pl.ds(R1, R2)], a2.at[me], loc_sem.at[1]),
        pltpu.make_async_copy(codes_hbm, codes, loc_sem.at[2]),
        pltpu.make_async_copy(scales_hbm, scales, loc_sem.at[3]),
        pltpu.make_async_copy(offsets_hbm, offsets, loc_sem.at[4]),
        pltpu.make_async_copy(lengths_hbm, lengths, loc_sem.at[5]),
        pltpu.make_async_copy(shard_map_hbm, shard_map, loc_sem.at[6]),
        pltpu.make_async_copy(
            teacher.at[:, pl.ds(pl.multiple_of(zh * NY * C, C), NY * C)], tz_land.at[zh], loc_sem.at[7]
        ),
    ]
    for c in loc:
        c.start()

    pl.semaphore_wait(barrier, 8)
    say_hello(0)
    loc[0].wait()
    loc[1].wait()

    def z1_full(d):
        src = slot_of(zh, y)
        return remote(a1.at[src], a1.at[src], a1s, z1r.at[d], z_nb[d])

    def z1_half(d):
        src = slot_of((zh + (NZ - 1 if d == 0 else 1)) % NZ, y)
        ref = a1.at[src, pl.ds(d * H1, H1)]
        return remote(ref, ref, a1s, z1r.at[2], z_nb[d])

    def y1_slot(s, k, d):
        off = k + k // 2 - 2 * (k // 3)
        yy = (y + NY - s) % NY if d == 0 else (y + s) % NY
        return slot_of((zh + off) % NZ, yy)

    def y1_full(s, k, d):
        ref = a1.at[y1_slot(s, k, d)]
        return remote(ref, ref, a1s, y1r.at[s, k], y_nb[d])

    def y1_half(k, d):
        ref = a1.at[y1_slot(3, k, d), pl.ds(d * H1, H1)]
        return remote(ref, ref, a1s, y1r.at[3, k], y_nb[d])

    def y2_slot(s, d):
        return slot_of(zh, (y + NY - s) % NY if d == 0 else (y + s) % NY)

    def y2_full(s, d):
        ref = a2.at[y2_slot(s, d)]
        return remote(ref, ref, a2s, y2r.at[s, d], y_nb[d])

    def y2_half(d):
        ref = a2.at[y2_slot(3, d), pl.ds(d * H2, H2)]
        return remote(ref, ref, a2s, y2hr, y_nb[d])

    def y_of(m):
        dist = (m + 1) // 2
        odd = m % 2
        return (y + NY + dist * (1 - 2 * odd)) % NY

    def z2_full(m, d):
        ref = a2.at[slot_of(zh, y_of(m))]
        return remote(ref, ref, a2s, z2r.at[m], z_nb[d])

    def z2_half(m, d):
        src = slot_of((zh + (NZ - 1 if d == 0 else 1)) % NZ, y_of(m))
        ref = a2.at[src, pl.ds(d * H2, H2)]
        return remote(ref, ref, a2s, z2hr.at[m], z_nb[d])

    for d in range(2):
        z1_full(d).start()
        y2_full(0, d).start()
        y1_full(0, 0, d).start()
        z2_full(0, d).start()

    def tz_copy(i):
        zt = (zh + i) % NZ
        return remote(
            teacher.at[:, pl.ds(pl.multiple_of(zt * NY * C, C), NY * C)], tz_land.at[zh],
            tzs, tzr, dev(zt, y),
        )

    def ty_copy(i):
        yt = (y + i) % NY
        return remote(
            tz_land.at[:, :, pl.ds(pl.multiple_of(yt * C, C), C)], t_land.at[y],
            tys, tyr, dev(zh, yt),
        )

    tz_copy(1).start()
    tz_copy(3).start()

    for c in loc[2:7]:
        c.wait()
    acc[...] = jnp.zeros_like(acc)
    rowsum[...] = jnp.zeros_like(rowsum)

    @pl.loop(0, GROUPS)
    def _(g):
        rows = pl.ds(pl.multiple_of(g * 128, 128), 128)
        weight[rows, :] = (
            codes[rows, :].astype(F32) * scales[pl.ds(g, 1), :] - offsets[pl.ds(g, 1), :]
        ).astype(BF16)

    group_iota = lax.broadcasted_iota(jnp.int32, (GROUPS, C), 0)
    feat_half = lax.broadcasted_iota(jnp.int32, (GROUPS, C), 1) // 128

    def use(a, slot, first, rows):
        at = pl.ds(first, rows)
        k0 = pl.ds(pl.multiple_of(slot * C, C), C)
        ka = pl.ds(pl.multiple_of(slot * C, C), 128)
        kb = pl.ds(pl.multiple_of(slot * C + 128, 128), 128)
        acc[at, :] += jnp.dot(a, weight[k0, :], preferred_element_type=F32)
        parts[2 * slot, at, :] = jnp.dot(a[:, :128], codes[ka, :], preferred_element_type=F32)
        parts[2 * slot + 1, at, :] = jnp.dot(a[:, 128:], codes[kb, :], preferred_element_type=F32)
        pick = (group_iota == 2 * slot + feat_half).astype(BF16)
        pad = jnp.zeros((T - rows, C), BF16)
        whole = jnp.concatenate([a, pad] if first == 0 else [pad, a], axis=0)
        rowsum[...] += lax.dot_general(
            pick, whole, (((1,), (1,)), ((), ())), preferred_element_type=F32
        )

    def use1(slot):
        use(a1[slot], slot, 0, R1)

    def use2(slot):
        use(a2[slot], slot, R1, R2)

    def make_target():
        wait_all(t_land.at[pl.ds(0, NY - 1)], tyr)
        own_t.wait()

        lane = lax.broadcasted_iota(jnp.int32, (8, T), 1)
        where_to = jnp.zeros((8, T), jnp.int32)
        for j in range(NT):
            where_to = jnp.where(
                lane // 8 == j % NY * NZ + j // NY, shard_map[j] * 8 + lane % 8, where_to
            )
        row = lax.broadcasted_iota(jnp.int32, (T, T), 0)
        perm = (row == where_to[:1, :]).astype(F32).astype(BF16)
        arrived = t_land[...].astype(F32).reshape(T, C).astype(BF16)
        target[...] = jnp.dot(perm, arrived, preferred_element_type=F32)

    own_t = pltpu.make_async_copy(
        tz_land.at[:, :, pl.ds(pl.multiple_of(y * C, C), C)], t_land.at[y], loc_sem.at[8]
    )

    def entry(table, n):
        value = jnp.int32(table[0])
        for i, item in enumerate(table):
            value = jnp.where(n == i, item, value)
        return value

    @pl.loop(0, len(PART1))
    def _(n):
        s = entry([e[0] for e in PART1], n)
        k = entry([e[1] for e in PART1], n)
        m, m1, m2 = entry(PART2_Y, n), entry(PART2_Z, n), entry(PART2_ZZ, n)

        @pl.when(s == 0)
        def _():
            @pl.when(k == 1)
            def _():
                z1_full(1).wait_recv()
                z1_half(1).start()

            @pl.when(k == 2)
            def _():
                z1_full(0).wait_recv()
                z1_half(0).start()

            @pl.when(k == 3)
            def _():
                wait_all(a1.at[0], z1r.at[2])

            @pl.when(k > 0)
            def _():
                y1_full(0, k, 0).start()
                y1_full(0, k, 1).start()

        for sv in (1, 2):
            @pl.when(s == sv)
            def _():
                wait_all(a1.at[pl.ds(0, 2)], y1r.at[sv - 1, k])
                for d in range(2):
                    y1_full(sv, k, d).start()

        @pl.when(s == 3)
        def _():
            wait_all(a1.at[pl.ds(0, 2)], y1r.at[2, k])
            for d in range(2):
                y1_half(k, d).start()

        @pl.when(s == 4)
        def _():
            wait_all(a1.at[0], y1r.at[3, k])

        @pl.when(m >= 1)
        def _():
            dist = (m + 1) // 2
            for d in range(2):
                @pl.when((m % 2 == 1 - d) & (m < 7))
                def _():
                    y2_full(dist - 1, d).wait_recv()

                    @pl.when(dist < 3)
                    def _():
                        y2_full(dist, d).start()

                    @pl.when(dist == 3)
                    def _():
                        y2_half(d).start()

            @pl.when(m == 7)
            def _():
                wait_all(a2.at[0], y2hr)

            z2_full(m, 0).start()
            z2_full(m, 1).start()

        @pl.when(m1 >= 0)
        def _():
            wait_all(a2.at[pl.ds(0, 2)], z2r.at[m1])
            for d in range(2):
                z2_half(m1, d).start()

        @pl.when(m2 >= 0)
        def _():
            wait_all(a2.at[0], z2hr.at[m2])

        use1(y1_slot(s, k, 0))

        @pl.when((s > 0) & (s < 4))
        def _():
            use1(y1_slot(s, k, 1))

        @pl.when(m >= 0)
        def _():
            use2(slot_of(zh, y_of(m)))

        @pl.when(m1 >= 0)
        def _():
            @pl.loop(0, 2)
            def _(d):
                use2(slot_of((zh + 1 + 2 * d) % NZ, y_of(m1)))

        @pl.when(m2 >= 0)
        def _():
            use2(slot_of((zh + 2) % NZ, y_of(m2)))

        for r in range(3):
            @pl.when(n == 3 + 3 * r)
            def _():
                hear_hello(r)
                if r < 2:
                    say_hello(r + 1)

        @pl.when(n == 8)
        def _():
            tz_copy(2).start()

        @pl.when(n == 12)
        def _():
            loc[7].wait()
            wait_all(tz_land.at[pl.ds(0, NZ - 1)], tzr)
            own_t.start()

            @pl.loop(1, NY)
            def _(i):
                ty_copy(i).start()

        @pl.when(n == 17)
        def _():
            make_target()

    total = lengths[0]
    for i in range(1, 32):
        total = total + lengths[i]
    token = lax.broadcasted_iota(jnp.int32, (T, C), 0)
    limit = jnp.where(token < SEQ, lengths[2 * dp], lengths[2 * dp + 1] + SEQ)
    live = (token < limit).astype(F32)
    cot16 = (2.0 * (acc[...] - target[...]) * live / total.astype(F32)).astype(BF16)
    acc[...] = cot16.astype(F32)

    rs = rowsum[...]
    hi = rs.astype(BF16)
    rest = rs - hi.astype(F32)
    mid = rest.astype(BF16)
    low = (rest - mid.astype(F32)).astype(BF16)
    offs = jnp.dot(hi, cot16, preferred_element_type=F32)
    offs += jnp.dot(mid, cot16, preferred_element_type=F32)
    offs += jnp.dot(low, cot16, preferred_element_type=F32)
    grads[pl.ds(8, 8)] = -offs.reshape(8, 8, C)

    def rs_copy(c):
        return remote(grads.at[c], rs_land.at[dp], rss, rsr, (c, me))

    @pl.loop(8, 16)
    def _(c):
        @pl.when(c != dp)
        def _():
            rs_copy(c).start()

    @pl.loop(0, 8)
    def _(c):
        for q in range(8):
            prod = parts[c * 8 + q] * acc[...]
            grads[c, pl.ds(q, 1), :] = jnp.sum(prod, axis=0, keepdims=True)

        @pl.when(c != dp)
        def _():
            rs_copy(c).start()

    rs_land[dp] = grads[dp]

    wait_all(rs_land.at[pl.ds(0, NDP - 1)], rsr)

    out[dp] = jnp.sum(rs_land[...], axis=0)

    def ag_copy(c):
        return remote(out.at[dp], out.at[dp], ags, agr, (c, me))

    @pl.loop(0, NDP)
    def _(c):
        @pl.when(c != dp)
        def _():
            ag_copy(c).start()

    wait_all(a1.at[pl.ds(0, NT - 1)], a1s)
    wait_all(a2.at[pl.ds(0, NT - 1)], a2s)
    wait_all(tz_land.at[pl.ds(0, NZ - 1)], tzs)
    wait_all(t_land.at[pl.ds(0, NY - 1)], tys)
    wait_all(rs_land.at[pl.ds(0, NDP - 1)], rss)
    wait_all(out.at[pl.ds(0, NDP - 1)], agr)
    wait_all(out.at[pl.ds(0, NDP - 1)], ags)


def per_device(attn_out, teacher, int_codes, scales, offsets, lengths, shard_map):
    dma = pltpu.SemaphoreType.DMA
    vmem = pl.BlockSpec(memory_space=pltpu.VMEM)
    hbm = pl.BlockSpec(memory_space=pltpu.HBM)
    out = pl.pallas_call(
        kernel,
        out_shape=pltpu.VMEM((NDP, 8, C), F32),
        in_specs=[hbm] * 7,
        out_specs=vmem,
        scratch_shapes=[
            pltpu.SMEM((32,), jnp.int32),
            pltpu.SMEM((32,), jnp.int32),
            pltpu.VMEM((GROUPS, C), F32),
            pltpu.VMEM((GROUPS, C), F32),
            pltpu.VMEM((NT, R1, C), BF16),
            pltpu.VMEM((NT, R2, C), BF16),
            pltpu.VMEM((8192, C), BF16),
            pltpu.VMEM((8192, C), BF16),
            pltpu.VMEM((GROUPS, T, C), F32),
            pltpu.VMEM((T, C), F32),
            pltpu.VMEM((GROUPS, T), F32),
            pltpu.VMEM((NZ, 8, NY * C), BF16),
            pltpu.VMEM((NY, NZ, 8, C), BF16),
            pltpu.VMEM((T, C), F32),
            pltpu.VMEM((NDP, 8, C), F32),
            pltpu.VMEM((NDP, 8, C), F32),
            dma((9,)),
            dma(()), dma(()),
            dma((4, 4)), dma((3,)),
            dma((3, 2)), dma(()),
            dma((8,)), dma((8,)),
            dma(()), dma(()), dma(()), dma(()),
            pltpu.SemaphoreType.REGULAR((3,)),
            dma(()), dma(()), dma(()), dma(()),
        ],
        compiler_params=pltpu.CompilerParams(
            collective_id=0, has_side_effects=True, vmem_limit_bytes=63 << 20
        ),
        cost_estimate=pl.CostEstimate(
            flops=3 * 2 * T * 8192 * C, bytes_accessed=6 << 20, transcendentals=0
        ),
    )(lengths, shard_map, attn_out, teacher, int_codes, scales, offsets)
    flat = out.reshape(128, C)
    return flat[:64], flat[64:]


def solution(mesh):
    in_specs = (
        P("dp", "tensor"),
        P(("dp", "tensor"), None),
        P(None, "tensor"),
        P(None, "tensor"),
        P(None, "tensor"),
        P(),
        P(),
    )
    out_specs = (P(None, "tensor"), P(None, "tensor"))
    return jax.shard_map(
        per_device, mesh=mesh, in_specs=in_specs, out_specs=out_specs, check_vma=False
    )
```

time: 79.5 us -> 67.4 us (0.85)
  local copies, waits for them, and re-layouts: 7.63 us -> 0.66 us
  Pallas kernels: 71 us -> 66 us
    unnamed x14 -> x0, local copies, waits for them, and re-layouts: 6.98 us -> none
    pallas_call x1, Pallas kernels: 71 us -> 66 us  [per_device(): pl.pallas_call(kernel, out_shape=pltpu.VMEM((NDP, 8, C), F32), in_specs=[...]
where the time goes in v2:
time: 67.4 us; the launch traced here: 67.3 us
  Pallas kernels  66 us (98%)
    pallas_call x1, Pallas kernels, per_device(): pl.pallas_call(kernel, out_shape=pltpu.VMEM((NDP, 8, C), F32), in_specs=[...  66 us

profile of v2, /device:TPU:1, one launch (start us, length us, event | category | flops | bytes accessed | tf_op | source)
XLA Modules:
  0.0 67.3 jit_solution(5104679187289798885)
XLA Ops:
  0.6 66.0 %shard_map.86 = f32[16,8,256]{2,1,0:T(8,128)S(1)} custom-call(s32[32]{0:T(128)} %lengths_hbm.1, s32[32]{0:T(128)} %shard_map_hbm.1, bf16[256,256]{1,0:T(8,128)(2,1)} %attn.1, bf16[8,8192]{1,0:T(8,128)(2,1)} %teacher.1, bf16[8192,256]{1,0:T(8,128)(2,1)} %codes_hbm.1, f32[64,256]{1,0:T(8,128)} %scales_hbm.1, f32[64,256]{1,0:T(8,128)} %offsets_hbm.1), custom_call_target="tpu_custom_call" | custom-call | flops 3221225472 | bytes 6291456 | tf_op jit(solution)/shard_map/pallas_call | solution.py:417
  66.7 0.7 slice_bitcast_fusion

commit v3 on v0

v3 whole, which is shorter than its diff:
```python
import jax
import jax.numpy as jnp
from jax import lax
from jax.experimental import pallas as pl
from jax.experimental.pallas import tpu as pltpu
from jax.sharding import PartitionSpec as P

SEQ = 128
T = 256
C = 256
NY, NZ = 8, 4
NT = NY * NZ
NDP = 16
GROUPS = 64
F32, BF16 = jnp.float32, jnp.bfloat16
MESH = pl.DeviceIdType.MESH
EVENTS = [
    (0, 0), (1, 0), (0, 1), (0, 2), (2, 0), (1, 1), (1, 2), (0, 3), (3, 0), (2, 1),
    (2, 2), (1, 3), (3, 1), (3, 2), (4, 0), (2, 3), (4, 1), (4, 2), (3, 3), (4, 3),
]
PIECE = [0, 1, 0, 2, 1, 3, 2, 4, 3, 5, 4, 6, 5, 7, 6, 7]
DIRECT = [1, 1, 0, 1, 0, 1, 0, 1, 0, 1, 0, 1, 0, 1, 0, 0]
LAG1, LAG2 = 4, 8
AHEAD = 3
HELLOS = 4


def entry(table, n):
    value = jnp.int32(table[0])
    for i, item in enumerate(table):
        value = jnp.where(n == i, item, value)
    return value


def kernel(
    lengths_hbm, shard_map_hbm, attn, teacher, codes_hbm, scales_hbm, offsets_hbm, out,
    lengths, shard_map, scales, offsets, a, codes, parts, acc, rowsum, tz, tf, t_land, target, grads, rs_land,
    loc, ays, acs, ayr, azr, acr, ws, w0r, wxr, whr, scs, scr,
    tps, tpr, tfr, tmr, tys, tyr, tcs, tcr, hello, rss, rsr, ags, agr,
):
    dp = lax.axis_index("dp")
    me = lax.axis_index("tensor")
    zh, y = me // NY, me % NY
    zl, x, core = dp // 8, dp // 2 % 4, dp % 2
    prim_core = zh // 2
    prim = core == prim_core
    sec = core != prim_core
    zp = 3 - zh
    zq = zh + 1 - 2 * (zh % 2)
    zr = 3 - zq

    def dev(zl_, x_, core_, zh_, y_):
        return (zl_ * 8 + x_ * 2 + core_, zh_ * NY + y_)

    y_nb = (dev(zl, x, core, zh, (y + 1) % NY), dev(zl, x, core, zh, (y + NY - 1) % NY))
    x_nb = (dev(zl, (x + 1) % 4, core, zh, y), dev(zl, (x + 3) % 4, core, zh, y))
    on_chip = dev(zl, x, 1 - core, zh, y)
    zl_nb = dev(1 - zl, x, core, zh, y)
    mate = dev(zl, x, core, zq, y)
    partner = dev(zl, x, core, zp, y)
    cross = dev(zl, x, 1 - core, zp, y)

    def remote(src, dst, ssem, rsem, to):
        return pltpu.make_async_remote_copy(
            src_ref=src, dst_ref=dst, send_sem=ssem, recv_sem=rsem,
            device_id=to, device_id_type=MESH,
        )

    def wait_all(ref, sem):
        pltpu.make_async_copy(ref, ref, sem).wait()

    barrier = pltpu.get_barrier_semaphore()
    for to in y_nb + x_nb + (on_chip, zl_nb, mate, partner, cross):
        pl.semaphore_signal(barrier, 1, device_id=to, device_id_type=MESH)

    def say_hello(r):
        for to in x_nb + (on_chip, zl_nb, cross):
            pl.semaphore_signal(hello.at[r], 1, device_id=to, device_id_type=MESH)

    def hear_hello(r):
        pl.semaphore_wait(hello.at[r], 5)
        if r + 1 < HELLOS:
            say_hello(r + 1)

    def plane_cols(z):
        return teacher.at[:, pl.ds(pl.multiple_of(z * NY * C, C), NY * C)]

    get_attn = pltpu.make_async_copy(attn, a.at[me], loc.at[0])
    get_codes = pltpu.make_async_copy(codes_hbm, codes, loc.at[1])
    get_scales = pltpu.make_async_copy(scales_hbm, scales, loc.at[2])
    get_offsets = pltpu.make_async_copy(offsets_hbm, offsets, loc.at[3])
    get_lengths = pltpu.make_async_copy(lengths_hbm, lengths, loc.at[4])
    get_map = pltpu.make_async_copy(shard_map_hbm, shard_map, loc.at[5])
    get_t = (
        pltpu.make_async_copy(plane_cols(zh), tz.at[0, zh], loc.at[6]),
        pltpu.make_async_copy(plane_cols(zp), tz.at[1, zh], loc.at[7]),
    )
    own_t = pltpu.make_async_copy(
        tz.at[:, :, :, pl.ds(pl.multiple_of(y * C, C), C)], t_land.at[:, y], loc.at[8]
    )

    @pl.when(prim)
    def _():
        for c in (get_attn, get_codes, get_scales, get_offsets) + get_t:
            c.start()

    get_lengths.start()
    get_map.start()
    acc[...] = jnp.zeros_like(acc)
    rowsum[...] = jnp.zeros_like(rowsum)
    pl.semaphore_wait(barrier, 9)

    group_iota = lax.broadcasted_iota(jnp.int32, (GROUPS, C), 0)
    feat_half = lax.broadcasted_iota(jnp.int32, (GROUPS, C), 1) // 128

    def use(slot):
        block = a[slot]
        halves = []
        for h in range(2):
            rows = pl.ds(pl.multiple_of(slot * C + h * 128, 128), 128)
            g = pl.ds(2 * slot + h, 1)
            piece = codes[rows, :]
            halves.append((piece.astype(F32) * scales[g, :] - offsets[g, :]).astype(BF16))
            parts[2 * slot + h] = jnp.dot(
                block[:, h * 128 : (h + 1) * 128], piece, preferred_element_type=F32
            )
        weight = jnp.concatenate(halves, axis=0)
        acc[...] += jnp.dot(block, weight, preferred_element_type=F32)
        pick = (group_iota == 2 * slot + feat_half).astype(BF16)
        rowsum[...] += lax.dot_general(
            pick, block, (((1,), (1,)), ((), ())), preferred_element_type=F32
        )

    def make_target():
        get_map.wait()
        lane = lax.broadcasted_iota(jnp.int32, (8, T), 1)
        where_to = jnp.zeros((8, T), jnp.int32)
        for j in range(NT):
            where_to = jnp.where(
                lane // 8 == j % NY * NZ + j // NY, shard_map[j] * 8 + lane % 8, where_to
            )
        row = lax.broadcasted_iota(jnp.int32, (T, T), 0)
        perm = (row == where_to[:1, :]).astype(F32).astype(BF16)
        arrived = t_land[0].astype(F32).reshape(T, C).astype(BF16)
        target[...] = jnp.dot(perm, arrived, preferred_element_type=F32)

    def slot_of(s, k, d):
        z = jnp.where(k == 0, zh, jnp.where(k == 1, zp, jnp.where(k == 2, zq, zr)))
        return z * NY + ((y + NY - s) % NY if d == 0 else (y + s) % NY)

    def y_full(s, k, d):
        ref = a.at[slot_of(s, k, d)]
        return remote(ref, ref, ays, ayr.at[s, k], y_nb[d])

    def y_half(k, d):
        ref = a.at[slot_of(3, k, d), pl.ds(d * 128, 128)]
        return remote(ref, ref, ays, ayr.at[3, k], y_nb[d])

    def share(s, k, d):
        ref = a.at[slot_of(s, k, d)]
        return remote(ref, ref, acs, acr.at[s, k], on_chip)

    def ty_copy(i):
        yt = (y + i) % NY
        return remote(
            tz.at[:, :, :, pl.ds(pl.multiple_of(yt * C, C), C)], t_land.at[:, y],
            tys, tyr, dev(zl, x, core, zh, yt),
        )

    def primary():
        get_attn.wait()
        remote(a.at[me], a.at[me], ays, azr.at[1], mate).start()
        for d in range(2):
            y_full(0, 0, d).start()
        share(0, 0, 0).start()
        remote(plane_cols(zq), tz.at[0, zh], tps, tmr, mate).start()
        remote(plane_cols(zr), tz.at[1, zh], tps, tmr, mate).start()
        get_codes.wait()
        get_scales.wait()
        get_offsets.wait()

        @pl.loop(0, len(EVENTS))
        def _(n):
            s = entry([e[0] for e in EVENTS], n)
            k = entry([e[1] for e in EVENTS], n)

            @pl.when(s == 0)
            def _():
                @pl.when(k == 1)
                def _():
                    wait_all(a.at[0], azr.at[0])
                    ref = a.at[slot_of(0, 1, 0)]
                    remote(ref, ref, ays, azr.at[2], mate).start()

                @pl.when(k > 1)
                def _():
                    wait_all(a.at[0], azr.at[k - 1])

                @pl.when(k > 0)
                def _():
                    y_full(0, k, 0).start()
                    y_full(0, k, 1).start()
                    share(0, k, 0).start()

            @pl.when((s > 0) & (s < 4))
            def _():
                wait_all(a.at[pl.ds(0, 2)], ayr.at[s - 1, k])
                for d in range(2):
                    @pl.when(s < 3)
                    def _():
                        y_full(s, k, d).start()

                    @pl.when(s == 3)
                    def _():
                        y_half(k, d).start()

                for d in range(2):
                    share(s, k, d).start()

            @pl.when(s == 4)
            def _():
                wait_all(a.at[0], ayr.at[3, k])
                share(4, k, 0).start()

            for r in range(HELLOS):
                @pl.when(n == 2 + 3 * r)
                def _():
                    hear_hello(r)

            @pl.when(n == 9)
            def _():
                wait_all(tf, tfr)
                remote(tf.at[0], tz.at[0, zp], tps, tmr, mate).start()
                remote(tf.at[1], tz.at[1, zp], tps, tmr, mate).start()

            @pl.when(n == 15)
            def _():
                for c in get_t:
                    c.wait()
                wait_all(tf, tpr)
                wait_all(tz.at[0], tmr)
                own_t.start()

                @pl.loop(1, NY)
                def _(i):
                    ty_copy(i).start()

            @pl.when(n == 18)
            def _():
                own_t.wait()
                wait_all(t_land.at[:, pl.ds(0, NY - 1)], tyr)
                remote(t_land.at[1], t_land.at[0], tcs, tcr, on_chip).start()

            use(slot_of(s, k, 0))

            @pl.when((s > 0) & (s < 4))
            def _():
                use(slot_of(s, k, 1))

        make_target()

    def y_of(m):
        return (y + NY + (m + 1) // 2 * (1 - 2 * (m % 2))) % NY

    def code_rows(q, m, h, first, count):
        return pl.ds(pl.multiple_of((q * NY + y_of(m)) * C + h * 128 + first, 64), count)

    def piece_of(e):
        m = entry(PIECE, e)
        direct = entry(DIRECT, e)
        return m, direct, jnp.where(direct == 1, zl, 1 - zl)

    def send_direct(m):
        rows = code_rows(x, m, zl, 0, 128)
        first = 2 * m - 1 + (m == 0) if isinstance(m, int) else 2 * m - 1
        remote(codes_hbm.at[rows], codes.at[rows], ws, w0r.at[first], cross).start()

    def secondary():
        remote(attn, a.at[me], ays, azr.at[0], partner).start()
        for m in range(AHEAD):
            send_direct(m)

        @pl.loop(0, 16 + LAG2)
        def _(n):
            @pl.when(n < 16)
            def _():
                m, direct, h = piece_of(n)
                rows = code_rows(x, m, h, 0, 128)
                wait_all(codes.at[pl.ds(0, 128)], w0r.at[n])
                for to in x_nb:
                    remote(codes.at[rows], codes.at[rows], ws, wxr.at[n], to).start()

                @pl.when(direct == 1)
                def _():
                    later = jnp.where(m < 7, 2 * m + 2, 15)
                    remote(codes.at[rows], codes.at[rows], ws, w0r.at[later], zl_nb).start()

                    @pl.when(m + AHEAD < NY)
                    def _():
                        send_direct(m + AHEAD)

            @pl.when(n == 3)
            def _():
                remote(scales_hbm, scales, scs.at[0], scr.at[0], cross).start()
                remote(offsets_hbm, offsets, scs.at[1], scr.at[1], cross).start()

            @pl.when(n == 6)
            def _():
                remote(plane_cols(zr), tf.at[0], tps, tfr, partner).start()
                remote(plane_cols(zq), tf.at[1], tps, tfr, partner).start()

            @pl.when(n == 9)
            def _():
                remote(plane_cols(zp), tz.at[0, zh], tps, tpr, partner).start()
                remote(plane_cols(zh), tz.at[1, zh], tps, tpr, partner).start()

            e1 = n - LAG1

            @pl.when((e1 >= 0) & (e1 < 16))
            def _():
                m, direct, h = piece_of(e1)
                wait_all(codes.at[pl.ds(0, 256)], wxr.at[e1])
                for d in range(2):
                    q = (x + 3) % 4 if d == 0 else (x + 1) % 4
                    rows = code_rows(q, m, h, d * 64, 64)
                    remote(codes.at[rows], codes.at[rows], ws, whr.at[e1], x_nb[d]).start()

            for r in range(HELLOS):
                @pl.when(n == 2 + 4 * r)
                def _():
                    hear_hello(r)

            e2 = n - LAG2

            @pl.when(e2 >= 0)
            def _():
                m, direct, h = piece_of(e2)
                wait_all(codes.at[pl.ds(0, 128)], whr.at[e2])

                @pl.when(direct == 0)
                def _():
                    s = (m + 1) // 2

                    @pl.when(m == 0)
                    def _():
                        wait_all(scales, scr.at[0])
                        wait_all(offsets, scr.at[1])

                    @pl.when((m == 0) | (m == 7))
                    def _():
                        @pl.loop(0, 4)
                        def _(k):
                            wait_all(a.at[0], acr.at[s, k])

                    @pl.when((m % 2 == 1) & (m < 7))
                    def _():
                        @pl.loop(0, 4)
                        def _(k):
                            wait_all(a.at[pl.ds(0, 2)], acr.at[s, k])

                    @pl.loop(0, 4)
                    def _(q):
                        use(q * NY + y_of(m))

        wait_all(t_land.at[0], tcr)
        make_target()

    say_hello(0)

    @pl.when(prim)
    def _():
        primary()

    @pl.when(sec)
    def _():
        secondary()

    get_lengths.wait()
    total = lengths[0]
    for i in range(1, 32):
        total = total + lengths[i]
    first_seq = 2 * (zl * 8 + x * 2 + prim_core)
    token = lax.broadcasted_iota(jnp.int32, (T, C), 0)
    limit = jnp.where(token < SEQ, lengths[first_seq], lengths[first_seq + 1] + SEQ)
    live = (token < limit).astype(F32)
    cot16 = (2.0 * (acc[...] - target[...]) * live / total.astype(F32)).astype(BF16)
    acc[...] = cot16.astype(F32)

    rs = rowsum[...]
    hi = rs.astype(BF16)
    rest = rs - hi.astype(F32)
    mid = rest.astype(BF16)
    low = (rest - mid.astype(F32)).astype(BF16)
    offs = jnp.dot(hi, cot16, preferred_element_type=F32)
    offs += jnp.dot(mid, cot16, preferred_element_type=F32)
    offs += jnp.dot(low, cot16, preferred_element_type=F32)
    grads[pl.ds(8, 8)] = -offs.reshape(8, 8, C)

    columns_at = jnp.where(prim, zh, zp) * NY + y
    giver = jnp.where(prim, 0, 8) + zl * 4 + x

    def rs_send(c):
        @pl.when(sec | (c != dp))
        def _():
            remote(grads.at[c], rs_land.at[giver], rss, rsr, (c, columns_at)).start()

    @pl.loop(8, 16)
    def _(c):
        rs_send(c)

    @pl.loop(0, 8)
    def _(c):
        for q in range(8):
            prod = parts[c * 8 + q] * acc[...]
            grads[c, pl.ds(q, 1), :] = jnp.sum(prod, axis=0, keepdims=True)
        rs_send(c)

    @pl.when(prim)
    def _():
        rs_land[giver] = grads[dp]
        wait_all(rs_land.at[pl.ds(0, NDP - 1)], rsr)

    @pl.when(sec)
    def _():
        wait_all(rs_land, rsr)

    out[dp] = jnp.sum(rs_land[...], axis=0)

    @pl.loop(0, NDP)
    def _(c):
        @pl.when(c != dp)
        def _():
            remote(out.at[dp], out.at[dp], ags, agr, (c, me)).start()

    wait_all(tz.at[0], tps)

    @pl.when(prim)
    def _():
        wait_all(a.at[pl.ds(0, 30)], ays)
        wait_all(a, acs)
        wait_all(t_land.at[:, pl.ds(0, NY - 1)], tys)
        wait_all(t_land.at[0], tcs)
        wait_all(rs_land.at[pl.ds(0, NDP - 1)], rss)

    @pl.when(sec)
    def _():
        wait_all(a.at[0], ays)
        wait_all(codes, ws)
        wait_all(scales, scs.at[0])
        wait_all(offsets, scs.at[1])
        wait_all(rs_land, rss)

    wait_all(out.at[pl.ds(0, NDP - 1)], ags)
    wait_all(out.at[pl.ds(0, NDP - 1)], agr)


def per_device(attn_out, teacher, int_codes, scales, offsets, lengths, shard_map):
    dma = pltpu.SemaphoreType.DMA
    hbm = pl.BlockSpec(memory_space=pltpu.HBM)
    out = pl.pallas_call(
        kernel,
        out_shape=pltpu.VMEM((NDP, 8, C), F32),
        in_specs=[hbm] * 7,
        out_specs=pl.BlockSpec(memory_space=pltpu.VMEM),
        scratch_shapes=[
            pltpu.SMEM((32,), jnp.int32),
            pltpu.SMEM((32,), jnp.int32),
            pltpu.VMEM((GROUPS, C), F32),
            pltpu.VMEM((GROUPS, C), F32),
            pltpu.VMEM((NT, T, C), BF16),
            pltpu.VMEM((NT * C, C), BF16),
            pltpu.VMEM((GROUPS, T, C), F32),
            pltpu.VMEM((T, C), F32),
            pltpu.VMEM((GROUPS, T), F32),
            pltpu.VMEM((2, NZ, 8, NY * C), BF16),
            pltpu.VMEM((2, 8, NY * C), BF16),
            pltpu.VMEM((2, NY, NZ, 8, C), BF16),
            pltpu.VMEM((T, C), F32),
            pltpu.VMEM((NDP, 8, C), F32),
            pltpu.VMEM((NDP, 8, C), F32),
            dma((9,)),
            dma(()), dma(()), dma((4, 4)), dma((3,)), dma((5, 4)),
            dma(()), dma((16,)), dma((16,)), dma((16,)), dma((2,)), dma((2,)),
            dma(()), dma(()), dma(()), dma(()), dma(()), dma(()), dma(()), dma(()),
            pltpu.SemaphoreType.REGULAR((HELLOS,)),
            dma(()), dma(()), dma(()), dma(()),
        ],
        compiler_params=pltpu.CompilerParams(
            collective_id=0, has_side_effects=True, vmem_limit_bytes=63 << 20
        ),
        cost_estimate=pl.CostEstimate(
            flops=3 * 2 * T * 8192 * C, bytes_accessed=6 << 20, transcendentals=0
        ),
    )(lengths, shard_map, attn_out, teacher, int_codes, scales, offsets)
    flat = out.reshape(128, C)
    return flat[:64], flat[64:]


def solution(mesh):
    in_specs = (
        P("dp", "tensor"),
        P(("dp", "tensor"), None),
        P(None, "tensor"),
        P(None, "tensor"),
        P(None, "tensor"),
        P(),
        P(),
    )
    out_specs = (P(None, "tensor"), P(None, "tensor"))
    return jax.shard_map(
        per_device, mesh=mesh, in_specs=in_specs, out_specs=out_specs, check_vma=False
    )
```

time: 392 us -> 65.1 us (0.17)
  waiting for transfers between devices: 324 us -> 0 us
  Pallas kernels: 0 us -> 63.7 us
  local copies, waits for them, and re-layouts: 21 us -> 0.66 us
  other arithmetic: 18.8 us -> 0 us
  between operations: 14.4 us -> 0.64 us
  matrix products: 12.4 us -> 0 us
    all_gather x2 -> x0, waiting for transfers between devices: 200 us -> none  [the longest x1 106 us: per_device(): lax.all_gather(attn_out, 'tensor', axis=1, tiled=True)]
    psum x1 -> x0, waiting for transfers between devices: 123 us -> none  [per_device(): grad_scale, grad_offset = lax.psum((part_scale, part_offset), 'dp')]
    pallas_call x0 -> x1, Pallas kernels: none -> 63.7 us  [per_device(): pl.pallas_call(kernel, out_shape=pltpu.VMEM((NDP, 8, C), F32), in_specs=[...]
    reduce_sum x3 -> x0, other arithmetic: 12.9 us -> none  [the longest x1 10.8 us: reduce_groups(): return (jnp.sum(shaped * codes_f, axis=1), -jnp.sum(shaped, axis=1))]
    dot_general x1 -> x0, matrix products: 12.4 us -> none  [per_device(): lax.dot_general(lax.all_gather(attn_out, 'tensor', axis=1, tiled=True), c...]
    unnamed x7 -> x0, local copies, waits for them, and re-layouts: 11.5 us -> none
    reshape x2 -> x0, local copies, waits for them, and re-layouts: 7.97 us -> none  [the longest x1 7.06 us: dequantize(): int_codes.astype(jnp.float32)]
    convert_element_type x1 -> x0, other arithmetic: 5.22 us -> none  [dequantize(): return (shaped * scales[:, None, :] - offsets[:, None, :]).reshape(in_row...]
  transfers between devices with their start and end apart: 3 -> 0, of which waited for: 3 -> 0; matrix products, arithmetic and copies ran while one was open for 4% -> 0% of each run, Pallas kernels for 0% -> 0%
where the time goes in v3:
time: 65.1 us; the launch traced here: 65 us
  Pallas kernels  63.7 us (98%)
  local copies, waits for them, and re-layouts  0.66 us (1%)
    pallas_call x1, Pallas kernels, per_device(): pl.pallas_call(kernel, out_shape=pltpu.VMEM((NDP, 8, C), F32), in_specs=[...  63.7 us

profile of v3, /device:TPU:1, one launch (start us, length us, event | category | flops | bytes accessed | tf_op | source)
XLA Modules:
  0.0 65.0 jit_solution(12828663953283714854)
XLA Ops:
  0.6 63.7 %shard_map.86 = f32[16,8,256]{2,1,0:T(8,128)S(1)} custom-call(s32[32]{0:T(128)} %lengths_hbm.1, s32[32]{0:T(128)} %shard_map_hbm.1, bf16[256,256]{1,0:T(8,128)(2,1)} %attn.1, bf16[8,8192]{1,0:T(8,128)(2,1)} %teacher.1, bf16[8192,256]{1,0:T(8,128)(2,1)} %codes_hbm.1, f32[64,256]{1,0:T(8,128)} %scales_hbm.1, f32[64,256]{1,0:T(8,128)} %offsets_hbm.1), custom_call_target="tpu_custom_call" | custom-call | flops 3221225472 | bytes 6291456 | tf_op jit(solution)/shard_map/pallas_call | solution.py:460
  64.3 0.7 %slice_bitcast_fusion = (f32[64,256]{1,0:T(8,128)}, f32[64,256]{1,0:T(8,128)}) fusion(f32[16,8,256]{2,1,0:T(8,128)S(1)} %shard_map.86), kind=kLoop, calls=%fused_computation | loop fusion | bytes 262144 | tf_op jit(solution)/shard_map/slice | solution.py:496

commit v4 on v3

--- a/solution.py
+++ b/solution.py
@@ -15,13 +15,16 @@
 F32, BF16 = jnp.float32, jnp.bfloat16
 MESH = pl.DeviceIdType.MESH
 EVENTS = [
-    (0, 0), (1, 0), (0, 1), (0, 2), (2, 0), (1, 1), (1, 2), (0, 3), (3, 0), (2, 1),
-    (2, 2), (1, 3), (3, 1), (3, 2), (4, 0), (2, 3), (4, 1), (4, 2), (3, 3), (4, 3),
+    0, 1, 8, 9, 4, 2, 5, 3, 12, 16, 10, 13, 6, 11, 7, 17, 20, 14, 18, 15,
+    21, 19, 22, 24, 25, 23, 28, 26, 29, 27, 30, 32, 33, 31, 36, 34, 37, 35, 38, 39,
 ]
 PIECE = [0, 1, 0, 2, 1, 3, 2, 4, 3, 5, 4, 6, 5, 7, 6, 7]
 DIRECT = [1, 1, 0, 1, 0, 1, 0, 1, 0, 1, 0, 1, 0, 1, 0, 0]
 LAG1, LAG2 = 4, 8
+BLOCK_AT = [-1] * 12 + [0, -1, 1, -1, 2, -1, 3, -1, 4, 5, 6, 7]
 AHEAD = 3
+TR_AT, TP_AT = 7, 9
+TY_AT, TC_AT = 28, 38
 HELLOS = 4
 
 
@@ -34,9 +37,9 @@
 
 def kernel(
     lengths_hbm, shard_map_hbm, attn, teacher, codes_hbm, scales_hbm, offsets_hbm, out,
-    lengths, shard_map, scales, offsets, a, codes, parts, acc, rowsum, tz, tf, t_land, target, grads, rs_land,
+    lengths, shard_map, scales, offsets, a, codes, parts, acc, rowsum, tz, t_land, target, grads, rs_land,
     loc, ays, acs, ayr, azr, acr, ws, w0r, wxr, whr, scs, scr,
-    tps, tpr, tfr, tmr, tys, tyr, tcs, tcr, hello, rss, rsr, ags, agr,
+    tps, tpr, tmr, tys, tyr, tcs, tcr, hello, rss, rsr, ags, agr,
 ):
     dp = lax.axis_index("dp")
     me = lax.axis_index("tensor")
@@ -69,16 +72,17 @@
     def wait_all(ref, sem):
         pltpu.make_async_copy(ref, ref, sem).wait()
 
+    near = y_nb + x_nb + (on_chip, zl_nb, mate, partner, cross)
     barrier = pltpu.get_barrier_semaphore()
-    for to in y_nb + x_nb + (on_chip, zl_nb, mate, partner, cross):
+    for to in near:
         pl.semaphore_signal(barrier, 1, device_id=to, device_id_type=MESH)
 
     def say_hello(r):
-        for to in x_nb + (on_chip, zl_nb, cross):
+        for to in near:
             pl.semaphore_signal(hello.at[r], 1, device_id=to, device_id_type=MESH)
 
     def hear_hello(r):
-        pl.semaphore_wait(hello.at[r], 5)
+        pl.semaphore_wait(hello.at[r], 9)
         if r + 1 < HELLOS:
             say_hello(r + 1)
 
@@ -144,17 +148,26 @@
         arrived = t_land[0].astype(F32).reshape(T, C).astype(BF16)
         target[...] = jnp.dot(perm, arrived, preferred_element_type=F32)
 
+    def plane_of(k):
+        return jnp.where(k == 0, zh, jnp.where(k == 1, zp, jnp.where(k == 2, zq, zr)))
+
+    def index_of(z):
+        return jnp.where(z == zh, 0, jnp.where(z == zp, 1, jnp.where(z == zq, 2, 3)))
+
     def slot_of(s, k, d):
-        z = jnp.where(k == 0, zh, jnp.where(k == 1, zp, jnp.where(k == 2, zq, zr)))
-        return z * NY + ((y + NY - s) % NY if d == 0 else (y + s) % NY)
-
-    def y_full(s, k, d):
-        ref = a.at[slot_of(s, k, d)]
-        return remote(ref, ref, ays, ayr.at[s, k], y_nb[d])
-
-    def y_half(k, d):
-        ref = a.at[slot_of(3, k, d), pl.ds(d * 128, 128)]
-        return remote(ref, ref, ays, ayr.at[3, k], y_nb[d])
+        return plane_of(k) * NY + ((y + NY - s) % NY if d == 0 else (y + s) % NY)
+
+    def half_of(s, kk, d):
+        return a.at[slot_of(s, kk // 2, d), pl.ds(pl.multiple_of(kk % 2 * 128, 128), 128)]
+
+    def y_full(s, kk, d):
+        ref = half_of(s, kk, d)
+        return remote(ref, ref, ays, ayr.at[s, kk], y_nb[d])
+
+    def y_part(kk, d):
+        rows = pl.ds(pl.multiple_of(kk % 2 * 128 + d * 64, 64), 64)
+        ref = a.at[slot_of(3, kk // 2, d), rows]
+        return remote(ref, ref, ays, ayr.at[3, kk], y_nb[d])
 
     def share(s, k, d):
         ref = a.at[slot_of(s, k, d)]
@@ -169,9 +182,11 @@
 
     def primary():
         get_attn.wait()
-        remote(a.at[me], a.at[me], ays, azr.at[1], mate).start()
-        for d in range(2):
-            y_full(0, 0, d).start()
+        for h in range(2):
+            ref = half_of(0, h, 0)
+            remote(ref, ref, ays, azr.at[1, h], mate).start()
+            for d in range(2):
+                y_full(0, h, d).start()
         share(0, 0, 0).start()
         remote(plane_cols(zq), tz.at[0, zh], tps, tmr, mate).start()
         remote(plane_cols(zr), tz.at[1, zh], tps, tmr, mate).start()
@@ -181,63 +196,63 @@
 
         @pl.loop(0, len(EVENTS))
         def _(n):
-            s = entry([e[0] for e in EVENTS], n)
-            k = entry([e[1] for e in EVENTS], n)
+            code = entry(EVENTS, n)
+            s, kk = code // 8, code % 8
+            k, h = kk // 2, kk % 2
 
             @pl.when(s == 0)
             def _():
-                @pl.when(k == 1)
-                def _():
-                    wait_all(a.at[0], azr.at[0])
-                    ref = a.at[slot_of(0, 1, 0)]
-                    remote(ref, ref, ays, azr.at[2], mate).start()
-
-                @pl.when(k > 1)
-                def _():
-                    wait_all(a.at[0], azr.at[k - 1])
-
                 @pl.when(k > 0)
                 def _():
-                    y_full(0, k, 0).start()
-                    y_full(0, k, 1).start()
-                    share(0, k, 0).start()
+                    wait_all(a.at[0, pl.ds(0, 128)], azr.at[k - 1, h])
+
+                    @pl.when(k == 1)
+                    def _():
+                        ref = half_of(0, kk, 0)
+                        remote(ref, ref, ays, azr.at[2, h], mate).start()
+
+                    y_full(0, kk, 0).start()
+                    y_full(0, kk, 1).start()
+
+                    @pl.when(h == 1)
+                    def _():
+                        share(0, k, 0).start()
 
             @pl.when((s > 0) & (s < 4))
             def _():
-                wait_all(a.at[pl.ds(0, 2)], ayr.at[s - 1, k])
+                wait_all(a.at[0], ayr.at[s - 1, kk])
                 for d in range(2):
                     @pl.when(s < 3)
                     def _():
-                        y_full(s, k, d).start()
+                        y_full(s, kk, d).start()
 
                     @pl.when(s == 3)
                     def _():
-                        y_half(k, d).start()
-
-                for d in range(2):
-                    share(s, k, d).start()
+                        y_part(kk, d).start()
+
+                @pl.when(h == 1)
+                def _():
+                    for d in range(2):
+                        share(s, k, d).start()
 
             @pl.when(s == 4)
             def _():
-                wait_all(a.at[0], ayr.at[3, k])
-                share(4, k, 0).start()
+                wait_all(a.at[0, pl.ds(0, 128)], ayr.at[3, kk])
+
+                @pl.when(h == 1)
+                def _():
+                    share(4, k, 0).start()
 
             for r in range(HELLOS):
-                @pl.when(n == 2 + 3 * r)
+                @pl.when(n == 4 + 6 * r)
                 def _():
                     hear_hello(r)
 
-            @pl.when(n == 9)
-            def _():
-                wait_all(tf, tfr)
-                remote(tf.at[0], tz.at[0, zp], tps, tmr, mate).start()
-                remote(tf.at[1], tz.at[1, zp], tps, tmr, mate).start()
-
-            @pl.when(n == 15)
+            @pl.when(n == TY_AT)
             def _():
                 for c in get_t:
                     c.wait()
-                wait_all(tf, tpr)
+                wait_all(tz.at[0, pl.ds(0, 2)], tpr)
                 wait_all(tz.at[0], tmr)
                 own_t.start()
 
@@ -245,19 +260,20 @@
                 def _(i):
                     ty_copy(i).start()
 
-            @pl.when(n == 18)
+            @pl.when(n == TC_AT)
             def _():
                 own_t.wait()
                 wait_all(t_land.at[:, pl.ds(0, NY - 1)], tyr)
                 remote(t_land.at[1], t_land.at[0], tcs, tcr, on_chip).start()
-
-            use(slot_of(s, k, 0))
-
-            @pl.when((s > 0) & (s < 4))
+                make_target()
+
+            @pl.when(h == 1)
+            def _():
+                use(slot_of(s, k, 0))
+
+            @pl.when((h == 1) & (s > 0) & (s < 4))
             def _():
                 use(slot_of(s, k, 1))
-
-        make_target()
 
     def y_of(m):
         return (y + NY + (m + 1) // 2 * (1 - 2 * (m % 2))) % NY
@@ -276,7 +292,9 @@
         remote(codes_hbm.at[rows], codes.at[rows], ws, w0r.at[first], cross).start()
 
     def secondary():
-        remote(attn, a.at[me], ays, azr.at[0], partner).start()
+        for h in range(2):
+            rows = pl.ds(h * 128, 128)
+            remote(attn.at[rows], a.at[me, rows], ays, azr.at[0, h], partner).start()
         for m in range(AHEAD):
             send_direct(m)
 
@@ -290,26 +308,49 @@
                 for to in x_nb:
                     remote(codes.at[rows], codes.at[rows], ws, wxr.at[n], to).start()
 
-                @pl.when(direct == 1)
-                def _():
-                    later = jnp.where(m < 7, 2 * m + 2, 15)
-                    remote(codes.at[rows], codes.at[rows], ws, w0r.at[later], zl_nb).start()
+                @pl.when((direct == 1) & (m < 7))
+                def _():
+                    remote(codes.at[rows], codes.at[rows], ws, w0r.at[2 * m + 2], zl_nb).start()
 
                     @pl.when(m + AHEAD < NY)
                     def _():
                         send_direct(m + AHEAD)
 
-            @pl.when(n == 3)
-            def _():
-                remote(scales_hbm, scales, scs.at[0], scr.at[0], cross).start()
-                remote(offsets_hbm, offsets, scs.at[1], scr.at[1], cross).start()
+                    @pl.when(m + AHEAD == 7)
+                    def _():
+                        last = code_rows(x, 7, zl, 0, 128)
+                        both = dev(1 - zl, x, 1 - core, zp, y)
+                        remote(codes_hbm.at[last], codes.at[last], ws, w0r.at[15], both).start()
+
+            @pl.when(n == 1)
+            def _():
+                @pl.when(zl == 0)
+                def _():
+                    remote(scales_hbm, scales, scs, scr.at[0], cross).start()
+
+                @pl.when(zl == 1)
+                def _():
+                    remote(offsets_hbm, offsets, scs, scr.at[1], cross).start()
 
             @pl.when(n == 6)
             def _():
-                remote(plane_cols(zr), tf.at[0], tps, tfr, partner).start()
-                remote(plane_cols(zq), tf.at[1], tps, tfr, partner).start()
-
-            @pl.when(n == 9)
+                @pl.when(zl == 0)
+                def _():
+                    wait_all(scales, scr.at[0])
+                    remote(scales, scales, scs, scr.at[0], zl_nb).start()
+
+                @pl.when(zl == 1)
+                def _():
+                    wait_all(offsets, scr.at[1])
+                    remote(offsets, offsets, scs, scr.at[1], zl_nb).start()
+
+            @pl.when(n == TR_AT)
+            def _():
+                other = dev(zl, x, core, zr, y)
+                remote(plane_cols(zr), tz.at[0, zh], tps, tmr, other).start()
+                remote(plane_cols(zq), tz.at[1, zh], tps, tmr, other).start()
+
+            @pl.when(n == TP_AT)
             def _():
                 remote(plane_cols(zp), tz.at[0, zh], tps, tpr, partner).start()
                 remote(plane_cols(zh), tz.at[1, zh], tps, tpr, partner).start()
@@ -330,40 +371,54 @@
                 def _():
                     hear_hello(r)
 
+            m = entry(BLOCK_AT, n)
+            s = (m + 1) // 2
+
+            @pl.when(m == 7)
+            def _():
+                wait_all(t_land.at[0], tcr)
+                make_target()
+
+                for i in (0, 1, 3):
+                    q = (x + i) % 4
+                    wait_all(a.at[0], acr.at[4, index_of(q)])
+                    use(q * NY + y_of(7))
+
             e2 = n - LAG2
 
             @pl.when(e2 >= 0)
             def _():
-                m, direct, h = piece_of(e2)
                 wait_all(codes.at[pl.ds(0, 128)], whr.at[e2])
 
-                @pl.when(direct == 0)
-                def _():
-                    s = (m + 1) // 2
-
+            @pl.when(m == 7)
+            def _():
+                q = (x + 2) % 4
+                wait_all(a.at[0], acr.at[4, index_of(q)])
+                use(q * NY + y_of(7))
+
+            @pl.when((m >= 0) & (m < 7))
+            def _():
+                @pl.when(m == 0)
+                def _():
+                    @pl.when(zl == 1)
+                    def _():
+                        wait_all(scales, scr.at[0])
+
+                    @pl.when(zl == 0)
+                    def _():
+                        wait_all(offsets, scr.at[1])
+
+                @pl.loop(0, 4)
+                def _(k):
                     @pl.when(m == 0)
                     def _():
-                        wait_all(scales, scr.at[0])
-                        wait_all(offsets, scr.at[1])
-
-                    @pl.when((m == 0) | (m == 7))
-                    def _():
-                        @pl.loop(0, 4)
-                        def _(k):
-                            wait_all(a.at[0], acr.at[s, k])
-
-                    @pl.when((m % 2 == 1) & (m < 7))
-                    def _():
-                        @pl.loop(0, 4)
-                        def _(k):
-                            wait_all(a.at[pl.ds(0, 2)], acr.at[s, k])
-
-                    @pl.loop(0, 4)
-                    def _(q):
-                        use(q * NY + y_of(m))
-
-        wait_all(t_land.at[0], tcr)
-        make_target()
+                        wait_all(a.at[0], acr.at[0, k])
+
+                    @pl.when(m % 2 == 1)
+                    def _():
+                        wait_all(a.at[pl.ds(0, 2)], acr.at[s, k])
+
+                    use(plane_of(k) * NY + y_of(m))
 
     say_hello(0)
 
@@ -432,10 +487,9 @@
         def _():
             remote(out.at[dp], out.at[dp], ags, agr, (c, me)).start()
 
-    wait_all(tz.at[0], tps)
-
     @pl.when(prim)
     def _():
+        wait_all(tz.at[0, pl.ds(0, 2)], tps)
         wait_all(a.at[pl.ds(0, 30)], ays)
         wait_all(a, acs)
         wait_all(t_land.at[:, pl.ds(0, NY - 1)], tys)
@@ -444,10 +498,10 @@
 
     @pl.when(sec)
     def _():
+        wait_all(tz.at[0], tps)
         wait_all(a.at[0], ays)
         wait_all(codes, ws)
-        wait_all(scales, scs.at[0])
-        wait_all(offsets, scs.at[1])
+        wait_all(target.at[pl.ds(0, 128)], scs)
         wait_all(rs_land, rss)
 
     wait_all(out.at[pl.ds(0, NDP - 1)], ags)
@@ -473,15 +527,14 @@
             pltpu.VMEM((T, C), F32),
             pltpu.VMEM((GROUPS, T), F32),
             pltpu.VMEM((2, NZ, 8, NY * C), BF16),
-            pltpu.VMEM((2, 8, NY * C), BF16),
             pltpu.VMEM((2, NY, NZ, 8, C), BF16),
             pltpu.VMEM((T, C), F32),
             pltpu.VMEM((NDP, 8, C), F32),
             pltpu.VMEM((NDP, 8, C), F32),
             dma((9,)),
-            dma(()), dma(()), dma((4, 4)), dma((3,)), dma((5, 4)),
-            dma(()), dma((16,)), dma((16,)), dma((16,)), dma((2,)), dma((2,)),
-            dma(()), dma(()), dma(()), dma(()), dma(()), dma(()), dma(()), dma(()),
+            dma(()), dma(()), dma((4, 8)), dma((3, 2)), dma((5, 4)),
+            dma(()), dma((16,)), dma((16,)), dma((16,)), dma(()), dma((2,)),
+            dma(()), dma(()), dma(()), dma(()), dma(()), dma(()), dma(()),
             pltpu.SemaphoreType.REGULAR((HELLOS,)),
             dma(()), dma(()), dma(()), dma(()),
         ],

time: 65.1 us -> 61.7 us (0.948)
  Pallas kernels: 63.7 us -> 60.3 us
    pallas_call x1, Pallas kernels: 63.7 us -> 60.3 us  [per_device(): pl.pallas_call(kernel, out_shape=pltpu.VMEM((NDP, 8, C), F32), in_specs=[...]
where the time goes in v4:
time: 61.7 us; the launch traced here: 61.6 us
  Pallas kernels  60.3 us (98%)
  local copies, waits for them, and re-layouts  0.66 us (1%)
  between operations  0.64 us (1%)
    pallas_call x1, Pallas kernels, per_device(): pl.pallas_call(kernel, out_shape=pltpu.VMEM((NDP, 8, C), F32), in_specs=[...  60.3 us

profile of v4, /device:TPU:1, one launch (start us, length us, event | category | flops | bytes accessed | tf_op | source)
XLA Modules:
  0.0 61.6 jit_solution(334316477055370491)
XLA Ops:
  0.6 60.3 %shard_map.86 = f32[16,8,256]{2,1,0:T(8,128)S(1)} custom-call(s32[32]{0:T(128)} %lengths_hbm.1, s32[32]{0:T(128)} %shard_map_hbm.1, bf16[256,256]{1,0:T(8,128)(2,1)} %attn.1, bf16[8,8192]{1,0:T(8,128)(2,1)} %teacher.1, bf16[8192,256]{1,0:T(8,128)(2,1)} %codes_hbm.1, f32[64,256]{1,0:T(8,128)} %scales_hbm.1, f32[64,256]{1,0:T(8,128)} %offsets_hbm.1), custom_call_target="tpu_custom_call" | custom-call | flops 3221225472 | bytes 6291456 | tf_op jit(solution)/shard_map/pallas_call | solution.py:514
  61.0 0.7 %slice_bitcast_fusion = (f32[64,256]{1,0:T(8,128)}, f32[64,256]{1,0:T(8,128)}) fusion(f32[16,8,256]{2,1,0:T(8,128)S(1)} %shard_map.86), kind=kLoop, calls=%fused_computation | loop fusion | bytes 262144 | tf_op jit(solution)/shard_map/slice | solution.py:549

commit v5 on v4

--- a/solution.py
+++ b/solution.py
@@ -24,7 +24,7 @@
 BLOCK_AT = [-1] * 12 + [0, -1, 1, -1, 2, -1, 3, -1, 4, 5, 6, 7]
 AHEAD = 3
 TR_AT, TP_AT = 7, 9
-TY_AT, TC_AT = 28, 38
+TY_AT, TC_AT = 26, 36
 HELLOS = 4
 
 
@@ -38,7 +38,7 @@
 def kernel(
     lengths_hbm, shard_map_hbm, attn, teacher, codes_hbm, scales_hbm, offsets_hbm, out,
     lengths, shard_map, scales, offsets, a, codes, parts, acc, rowsum, tz, t_land, target, grads, rs_land,
-    loc, ays, acs, ayr, azr, acr, ws, w0r, wxr, whr, scs, scr,
+    loc, ays, acs, qr, acr, ws, scs, scr,
     tps, tpr, tmr, tys, tyr, tcs, tcr, hello, rss, rsr, ags, agr,
 ):
     dp = lax.axis_index("dp")
@@ -162,12 +162,12 @@
 
     def y_full(s, kk, d):
         ref = half_of(s, kk, d)
-        return remote(ref, ref, ays, ayr.at[s, kk], y_nb[d])
+        return remote(ref, ref, ays, qr.at[s * 8 + kk], y_nb[d])
 
     def y_part(kk, d):
         rows = pl.ds(pl.multiple_of(kk % 2 * 128 + d * 64, 64), 64)
         ref = a.at[slot_of(3, kk // 2, d), rows]
-        return remote(ref, ref, ays, ayr.at[3, kk], y_nb[d])
+        return remote(ref, ref, ays, qr.at[24 + kk], y_nb[d])
 
     def share(s, k, d):
         ref = a.at[slot_of(s, k, d)]
@@ -184,7 +184,7 @@
         get_attn.wait()
         for h in range(2):
             ref = half_of(0, h, 0)
-            remote(ref, ref, ays, azr.at[1, h], mate).start()
+            remote(ref, ref, ays, qr.at[34 + h], mate).start()
             for d in range(2):
                 y_full(0, h, d).start()
         share(0, 0, 0).start()
@@ -204,12 +204,12 @@
             def _():
                 @pl.when(k > 0)
                 def _():
-                    wait_all(a.at[0, pl.ds(0, 128)], azr.at[k - 1, h])
+                    wait_all(a.at[0, pl.ds(0, 128)], qr.at[30 + 2 * k + h])
 
                     @pl.when(k == 1)
                     def _():
                         ref = half_of(0, kk, 0)
-                        remote(ref, ref, ays, azr.at[2, h], mate).start()
+                        remote(ref, ref, ays, qr.at[36 + h], mate).start()
 
                     y_full(0, kk, 0).start()
                     y_full(0, kk, 1).start()
@@ -220,7 +220,7 @@
 
             @pl.when((s > 0) & (s < 4))
             def _():
-                wait_all(a.at[0], ayr.at[s - 1, kk])
+                wait_all(a.at[0], qr.at[(s - 1) * 8 + kk])
                 for d in range(2):
                     @pl.when(s < 3)
                     def _():
@@ -237,7 +237,7 @@
 
             @pl.when(s == 4)
             def _():
-                wait_all(a.at[0, pl.ds(0, 128)], ayr.at[3, kk])
+                wait_all(a.at[0, pl.ds(0, 128)], qr.at[24 + kk])
 
                 @pl.when(h == 1)
                 def _():
@@ -289,12 +289,12 @@
     def send_direct(m):
         rows = code_rows(x, m, zl, 0, 128)
         first = 2 * m - 1 + (m == 0) if isinstance(m, int) else 2 * m - 1
-        remote(codes_hbm.at[rows], codes.at[rows], ws, w0r.at[first], cross).start()
+        remote(codes_hbm.at[rows], codes.at[rows], ws, qr.at[first], cross).start()
 
     def secondary():
         for h in range(2):
             rows = pl.ds(h * 128, 128)
-            remote(attn.at[rows], a.at[me, rows], ays, azr.at[0, h], partner).start()
+            remote(attn.at[rows], a.at[me, rows], ays, qr.at[32 + h], partner).start()
         for m in range(AHEAD):
             send_direct(m)
 
@@ -304,13 +304,13 @@
             def _():
                 m, direct, h = piece_of(n)
                 rows = code_rows(x, m, h, 0, 128)
-                wait_all(codes.at[pl.ds(0, 128)], w0r.at[n])
+                wait_all(codes.at[pl.ds(0, 128)], qr.at[n])
                 for to in x_nb:
-                    remote(codes.at[rows], codes.at[rows], ws, wxr.at[n], to).start()
+                    remote(codes.at[rows], codes.at[rows], ws, qr.at[16 + n], to).start()
 
                 @pl.when((direct == 1) & (m < 7))
                 def _():
-                    remote(codes.at[rows], codes.at[rows], ws, w0r.at[2 * m + 2], zl_nb).start()
+                    remote(codes.at[rows], codes.at[rows], ws, qr.at[2 * m + 2], zl_nb).start()
 
                     @pl.when(m + AHEAD < NY)
                     def _():
@@ -320,7 +320,7 @@
                     def _():
                         last = code_rows(x, 7, zl, 0, 128)
                         both = dev(1 - zl, x, 1 - core, zp, y)
-                        remote(codes_hbm.at[last], codes.at[last], ws, w0r.at[15], both).start()
+                        remote(codes_hbm.at[last], codes.at[last], ws, qr.at[15], both).start()
 
             @pl.when(n == 1)
             def _():
@@ -360,11 +360,11 @@
             @pl.when((e1 >= 0) & (e1 < 16))
             def _():
                 m, direct, h = piece_of(e1)
-                wait_all(codes.at[pl.ds(0, 256)], wxr.at[e1])
+                wait_all(codes.at[pl.ds(0, 256)], qr.at[16 + e1])
                 for d in range(2):
                     q = (x + 3) % 4 if d == 0 else (x + 1) % 4
                     rows = code_rows(q, m, h, d * 64, 64)
-                    remote(codes.at[rows], codes.at[rows], ws, whr.at[e1], x_nb[d]).start()
+                    remote(codes.at[rows], codes.at[rows], ws, qr.at[32 + e1], x_nb[d]).start()
 
             for r in range(HELLOS):
                 @pl.when(n == 2 + 4 * r)
@@ -388,7 +388,7 @@
 
             @pl.when(e2 >= 0)
             def _():
-                wait_all(codes.at[pl.ds(0, 128)], whr.at[e2])
+                wait_all(codes.at[pl.ds(0, 128)], qr.at[32 + e2])
 
             @pl.when(m == 7)
             def _():
@@ -459,12 +459,16 @@
         def _():
             remote(grads.at[c], rs_land.at[giver], rss, rsr, (c, columns_at)).start()
 
-    @pl.loop(8, 16)
-    def _(c):
-        rs_send(c)
+    def in_order(i):
+        return (x + entry([2, 1, 3, 0], i // 2)) % 4 * 2 + (core + 1 + i) % 2
 
     @pl.loop(0, 8)
-    def _(c):
+    def _(i):
+        rs_send(8 + in_order(i))
+
+    @pl.loop(0, 8)
+    def _(i):
+        c = in_order(i)
         for q in range(8):
             prod = parts[c * 8 + q] * acc[...]
             grads[c, pl.ds(q, 1), :] = jnp.sum(prod, axis=0, keepdims=True)
@@ -481,11 +485,12 @@
 
     out[dp] = jnp.sum(rs_land[...], axis=0)
 
-    @pl.loop(0, NDP)
-    def _(c):
-        @pl.when(c != dp)
-        def _():
-            remote(out.at[dp], out.at[dp], ags, agr, (c, me)).start()
+    for dx in (2, 1, 3, 0):
+        for dz in (1, 0):
+            for dc in (1, 0):
+                if dx + dz + dc > 0:
+                    to = dev((zl + dz) % 2, (x + dx) % 4, (core + dc) % 2, zh, y)
+                    remote(out.at[dp], out.at[dp], ags, agr, to).start()
 
     @pl.when(prim)
     def _():
@@ -532,8 +537,8 @@
             pltpu.VMEM((NDP, 8, C), F32),
             pltpu.VMEM((NDP, 8, C), F32),
             dma((9,)),
-            dma(()), dma(()), dma((4, 8)), dma((3, 2)), dma((5, 4)),
-            dma(()), dma((16,)), dma((16,)), dma((16,)), dma(()), dma((2,)),
+            dma(()), dma(()), dma((48,)), dma((5, 4)),
+            dma(()), dma(()), dma((2,)),
             dma(()), dma(()), dma(()), dma(()), dma(()), dma(()), dma(()),
             pltpu.SemaphoreType.REGULAR((HELLOS,)),
             dma(()), dma(()), dma(()), dma(()),

time: 61.7 us -> 61 us (0.989)
  Pallas kernels: 60.3 us -> 59.6 us
    pallas_call x1, Pallas kernels: 60.3 us -> 59.6 us  [per_device(): pl.pallas_call(kernel, out_shape=pltpu.VMEM((NDP, 8, C), F32), in_specs=[...]
where the time goes in v5:
time: 61 us; the launch traced here: 60.9 us
  Pallas kernels  59.6 us (98%)
  local copies, waits for them, and re-layouts  0.66 us (1%)
  between operations  0.64 us (1%)
    pallas_call x1, Pallas kernels, per_device(): pl.pallas_call(kernel, out_shape=pltpu.VMEM((NDP, 8, C), F32), in_specs=[...  59.6 us

profile of v5, /device:TPU:1, one launch (start us, length us, event | category | flops | bytes accessed | tf_op | source)
XLA Modules:
  0.0 60.9 jit_solution(17924485756447621399)
XLA Ops:
  0.6 59.6 %shard_map.86 = f32[16,8,256]{2,1,0:T(8,128)S(1)} custom-call(s32[32]{0:T(128)} %lengths_hbm.1, s32[32]{0:T(128)} %shard_map_hbm.1, bf16[256,256]{1,0:T(8,128)(2,1)} %attn.1, bf16[8,8192]{1,0:T(8,128)(2,1)} %teacher.1, bf16[8192,256]{1,0:T(8,128)(2,1)} %codes_hbm.1, f32[64,256]{1,0:T(8,128)} %scales_hbm.1, f32[64,256]{1,0:T(8,128)} %offsets_hbm.1), custom_call_target="tpu_custom_call" | custom-call | flops 3221225472 | bytes 6291456 | tf_op jit(solution)/shard_map/pallas_call | solution.py:519
  60.2 0.7 %slice_bitcast_fusion = (f32[64,256]{1,0:T(8,128)}, f32[64,256]{1,0:T(8,128)}) fusion(f32[16,8,256]{2,1,0:T(8,128)S(1)} %shard_map.86), kind=kLoop, calls=%fused_computation | loop fusion | bytes 262144 | tf_op jit(solution)/shard_map/slice | solution.py:554

commit v6 on v5

--- a/solution.py
+++ b/solution.py
@@ -295,7 +295,8 @@
         for h in range(2):
             rows = pl.ds(h * 128, 128)
             remote(attn.at[rows], a.at[me, rows], ays, qr.at[32 + h], partner).start()
-        for m in range(AHEAD):
+            send_direct(h)
+        for m in range(2, AHEAD):
             send_direct(m)
 
         @pl.loop(0, 16 + LAG2)

time: 61 us -> 61.9 us (1.015)
  Pallas kernels: 59.6 us -> 60.5 us
    pallas_call x1, Pallas kernels: 59.6 us -> 60.5 us  [per_device(): pl.pallas_call(kernel, out_shape=pltpu.VMEM((NDP, 8, C), F32), in_specs=[...]
where the time goes in v6:
time: 61.9 us; the launch traced here: 61.8 us
  Pallas kernels  60.5 us (98%)
  local copies, waits for them, and re-layouts  0.66 us (1%)
  between operations  0.64 us (1%)
    pallas_call x1, Pallas kernels, per_device(): pl.pallas_call(kernel, out_shape=pltpu.VMEM((NDP, 8, C), F32), in_specs=[...  60.5 us

profile of v6, /device:TPU:1, one launch (start us, length us, event | category | flops | bytes accessed | tf_op | source)
XLA Modules:
  0.0 61.8 jit_solution(9832904610352254428)
XLA Ops:
  0.6 60.5 %shard_map.86 = f32[16,8,256]{2,1,0:T(8,128)S(1)} custom-call(s32[32]{0:T(128)} %lengths_hbm.1, s32[32]{0:T(128)} %shard_map_hbm.1, bf16[256,256]{1,0:T(8,128)(2,1)} %attn.1, bf16[8,8192]{1,0:T(8,128)(2,1)} %teacher.1, bf16[8192,256]{1,0:T(8,128)(2,1)} %codes_hbm.1, f32[64,256]{1,0:T(8,128)} %scales_hbm.1, f32[64,256]{1,0:T(8,128)} %offsets_hbm.1), custom_call_target="tpu_custom_call" | custom-call | flops 3221225472 | bytes 6291456 | tf_op jit(solution)/shard_map/pallas_call | solution.py:520
  61.1 0.7 %slice_bitcast_fusion = (f32[64,256]{1,0:T(8,128)}, f32[64,256]{1,0:T(8,128)}) fusion(f32[16,8,256]{2,1,0:T(8,128)S(1)} %shard_map.86), kind=kLoop, calls=%fused_computation | loop fusion | bytes 262144 | tf_op jit(solution)/shard_map/slice | solution.py:555
